TPU v7x, 32 devices: a whole 2x2x4 slice. The times are simulated.
32 devices in a mesh: groups: 2 (over y), store: 16 (over z, x, core).
Axes of the slice: x: 2, y: 2, z: 4, core: 2. Of those that a mesh axis runs over, the one named last changes fastest.
Arguments:
- tokens: bfloat16 [32768, 8192], P('groups', 'store'), parts along dimension 0, may hold values from -6 to 6
- up_grad: bfloat16 [32768, 28672], P('groups', 'store'), parts along dimension 0, may hold values from -6 to 6
- in_index: int32 [8, 32], replicated, may hold values from 0 to 255
- in_values: bfloat16 [8, 32, 32, 8], replicated, may hold values from -0.1875 to 0.1875
- out_index: int32 [8, 112], replicated, may hold values from 0 to 895
- out_values: bfloat16 [8, 112, 32, 8], replicated, may hold values from -0.09375 to 0.09375
- stored: bfloat16 [8192, 4096], P(('groups', 'store')), parts along dimension 0, may hold values from -6 to 6
Outputs:
- scores: float32 [8, 4096], P('groups', 'store'), parts along dimension 0
There are 2 independent parts, one for each index of `groups`. A program takes and returns all parts, laid end to end along the dimension named above; an argument that names none is the same for every part. Nothing has to cross between parts.
All inputs are finite; a program needn't handle non-finite values.
Results may differ from a plain program's by a relative error of at most 0.0034.
Values sent between devices are 32-bit elements; how exact they have to be, the bound alone decides.
No kernel may reach another device: no remote copies, remote signals or barrier semaphores. Data moves between devices by JAX's collectives and lax.ppermute only.
A program may use at most 192 MiB of HBM per device.

v0:
```python
import jax
import jax.numpy as jnp
from jax import lax
from jax.sharding import PartitionSpec as P

LEN = 4096
BLOCK = 32


def dense_projection(index, values, first, count):
    blocks = first + jnp.arange(count, dtype=jnp.int32)
    onehot = (index[:, :, None] == blocks[None, None, :]).astype(jnp.float32)
    dense = jnp.einsum("ckn,ckrw->nrcw", onehot, values.astype(jnp.float32))
    return dense.reshape(count * values.shape[2], values.shape[0] * values.shape[3]).astype(
        jnp.bfloat16
    )


def on_device(tokens, up_grad, in_index, in_values, out_index, out_values, stored):
    rank = lax.axis_index("store")
    tok_rows = tokens.shape[0]
    feat_blocks = tokens.shape[1] // BLOCK
    hidden_blocks = up_grad.shape[1] // BLOCK
    width = in_values.shape[0] * in_values.shape[3]
    seq_count = tok_rows // LEN
    in_proj = dense_projection(in_index, in_values, rank * feat_blocks, feat_blocks)
    out_proj = dense_projection(out_index, out_values, rank * hidden_blocks, hidden_blocks)
    in_part = jnp.dot(tokens, in_proj, preferred_element_type=jnp.float32)
    out_part = jnp.dot(up_grad, out_proj, preferred_element_type=jnp.float32)
    inputs, outputs = lax.psum((in_part, out_part), "store")
    left = inputs.reshape(seq_count, LEN, width)
    right = outputs.reshape(seq_count, LEN, width)
    example = jnp.einsum("slp,slq->spq", left, right, precision=lax.Precision.HIGHEST) / LEN
    example_grad = example.reshape(seq_count, width * width).astype(jnp.bfloat16)
    return lax.dot_general(
        example_grad, stored, (((1,), (1,)), ((), ())), preferred_element_type=jnp.float32
    )


def solution(mesh):
    return jax.shard_map(
        on_device,
        mesh=mesh,
        in_specs=(
            P("groups", "store"),
            P("groups", "store"),
            P(),
            P(),
            P(),
            P(),
            P(("groups", "store"), None),
        ),
        out_specs=P("groups", "store"),
        check_vma=False,
    )
```

profile of v0, /device:TPU:0, one launch (start us, length us, event | category | flops | bytes accessed | tf_op | source)
XLA Modules:
  0.0 247.2 jit_solution(4227786089813507648)
XLA Ops:
  6.5 0.0 copy-start
  6.5 0.0 all-reduce.3.cloned.1.call-start
  6.5 1.5 fusion.1
  8.0 0.8 convert_element_type.30
  8.9 1.4 fusion
  10.3 0.4 copy.15
  10.7 0.5 convert_element_type.33
  11.3 0.0 copy-start.1
  11.3 26.6 %fusion.14 = f32[64,16384]{1,0:T(8,128)} fusion(bf16[1792,64]{0,1:T(8,128)(2,1)S(1)} %convert_element_type.33, bf16[16384,1792]{1,0:T(8,128)(2,1)} %param.8), kind=kOutput, calls=%fused_computation.21 | convolution fusion | flops 3758096384 | bytes 63143936 | tf_op jit(solution)/shard_map/dot_general | solution.py:29
  37.9 0.0 copy-done.1
  37.9 12.8 %fusion.13 = f32[64,16384]{1,0:T(8,128)} fusion(bf16[512,64]{0,1:T(8,128)(2,1)S(1)} %copy-done.1, bf16[16384,512]{1,0:T(8,128)(2,1)} %param.7), kind=kOutput, calls=%fused_computation.20 | convolution fusion | flops 1073741824 | bytes 21037056 | tf_op jit(solution)/shard_map/dot_general | solution.py:28
  50.7 7.7 %copy_bitcast_fusion = (f32[4,4096,64]{1,2,0:T(8,128)}, f32[4,4096,64]{1,2,0:T(8,128)}) fusion(f32[8,4,8,4096]{3,2,1,0:T(8,128)} %bitcast.38, f32[8,4,8,4096]{3,2,1,0:T(8,128)} %bitcast.39), kind=kLoop, calls=%fused_computation | loop fusion | bytes 16777216 | tf_op jit(solution)/shard_map/reshape | solution.py:32
  58.4 0.0 all-reduce.3.cloned.1.call-update
  58.5 173.2 %all-reduce.3.cloned.1.call-done = (f32[4,4096,64]{1,2,0:T(8,128)}, f32[4,4096,64]{1,2,0:T(8,128)}) async-done(((f32[4,4096,64]{1,2,0:T(8,128)}, f32[4,4096,64]{1,2,0:T(8,128)}), (f32[4,4096,64]{1,2,0:T(8,128)}, f32[4,4096,64]{1,2,0:T(8,128)})) %all-reduce.3.cloned.1.call-update) | async-done | bytes 8388624 | tf_op jit(solution)/shard_map/psum | solution.py:30
  231.6 7.4 %fusion.2 = bf16[4,64,64]{2,1,0:T(8,128)(2,1)S(1)} fusion(f32[4,4096,64]{1,2,0:T(8,128)} %get-tuple-element.5, f32[4,4096,64]{1,2,0:T(8,128)} %get-tuple-element.6), kind=kOutput, calls=%fused_computation.7 | convolution fusion | flops 805339136 | bytes 8421376 | tf_op jit(solution)/shard_map/slp,slq->spq/dot_general | solution.py:33
  239.0 0.1 convert_element_type.35
  239.1 0.0 copy-done
  239.1 1.2 fusion.15
  (2 shorter events, 0.0 us)
Async XLA Ops:
  6.5 232.6 %copy-start = (bf16[256,4096]{1,0:T(8,128)(2,1)S(1)}, bf16[256,4096]{1,0:T(8,128)(2,1)}, u32[]{:S(2)}) copy-start(bf16[256,4096]{1,0:T(8,128)(2,1)} %param.13) | copy-start | bytes 6291460
  6.5 225.1 %all-reduce.3.cloned.1.call-start = ((), (), s32[]{:S(2)}) async-start(), calls=%async_computation | async-start | bytes 16777216 | tf_op jit(solution)/shard_map/psum | solution.py:30
  11.3 26.6 %copy-start.1 = (bf16[512,64]{0,1:T(8,128)(2,1)S(1)}, bf16[512,64]{0,1:T(8,128)(2,1)}, u32[]{:S(2)}) copy-start(bf16[512,64]{0,1:T(8,128)(2,1)} %convert_element_type.30) | copy-start | bytes 196612
Sparse Core Ops, SparseCore 0:
  58.6 172.9 all-reduce.2
where the time goes:
time: 247 us
  waiting for transfers between devices  173 us (70%)
  matrix products  51 us (21%)
  between operations  13.5 us (5%)
  local copies, waits for them, and re-layouts  9.61 us (4%)
    psum x1, waiting for transfers between devices, on_device(): inputs, outputs = lax.psum((in_part, out_part), 'store')  173 us
    dot_general x1, matrix products, on_device(): out_part = jnp.dot(up_grad, out_proj, preferred_element_type=jnp.float32)  26.6 us
    dot_general x1, matrix products, on_device(): in_part = jnp.dot(tokens, in_proj, preferred_element_type=jnp.float32)  12.8 us
    reshape x1, local copies, waits for them, and re-layouts, on_device(): right = outputs.reshape(seq_count, LEN, width)  7.69 us
    dot_general x1, matrix products, on_device(): jnp.einsum('slp,slq->spq', left, right, precision=lax.Precision.HIGHEST)  7.38 us
  transfers between devices with their start and end apart: 1, of which 1 were waited for; matrix products, arithmetic and copies ran while one was open for 0% of the time, Pallas kernels for 0%

commit v1 on v0

v1 whole, which is shorter than its diff:
```python
import functools

import jax
import jax.numpy as jnp
from jax import lax
from jax.experimental import pallas as pl
from jax.experimental.pallas import tpu as pltpu
from jax.sharding import PartitionSpec as P

LEN = 4096
BLOCK = 32
LANES = 128
HALF = LANES // 2
SLOTS = 4
VMEM_LIMIT = 16 * 1024 * 1024

ANY = pl.BlockSpec(memory_space=pl.ANY)
IN_HBM = pl.BlockSpec(memory_space=pltpu.HBM)
IN_VMEM = pl.BlockSpec(memory_space=pltpu.VMEM)
IN_SMEM = pl.BlockSpec(memory_space=pltpu.SMEM)
PARAMS = pltpu.CompilerParams(vmem_limit_bytes=VMEM_LIMIT)


def build_in(first, index_ref, values_ref, w_ref, list_ref, acc_ref):
    groups, picks = index_ref.shape
    cwidth = values_ref.shape[1]
    count = acc_ref.shape[0]
    acc_ref[...] = jnp.zeros_like(acc_ref)
    found = jnp.int32(0)
    for c in range(groups):

        def scan(k, found, c=c):
            block = index_ref[c, k] - first
            list_ref[0, found] = c * picks + k
            list_ref[1, found] = block
            list_ref[2, found] = c * cwidth
            return found + jnp.where((block >= 0) & (block < count), 1, 0).astype(jnp.int32)

        found = lax.fori_loop(0, picks, scan, found, unroll=8)

    def add(i, carry):
        rows = pl.ds(pl.multiple_of(list_ref[2, i], cwidth), cwidth)
        acc_ref[list_ref[1, i], rows, :BLOCK] += values_ref[list_ref[0, i]].astype(jnp.float32)
        return carry

    lax.fori_loop(0, found, add, jnp.int32(0))
    for n in range(count):
        block = acc_ref[n]
        wide = jnp.concatenate([block, jnp.zeros_like(block)], axis=0).T[:BLOCK]
        rows = slice(n * BLOCK, (n + 1) * BLOCK)
        w_ref[0, rows] = wide.astype(jnp.bfloat16)
        w_ref[1, rows] = pltpu.roll(wide, HALF, 1).astype(jnp.bfloat16)


def build_out_kernel(count, first_ref, index_ref, values_ref, *rest):
    w_ref, by_block_ref, wide_ref = rest[-3:]
    groups, picks = index_ref.shape
    cwidth = values_ref.shape[1] // BLOCK
    ids = lax.broadcasted_iota(jnp.int32, (LANES, picks), 0) + first_ref[0]
    for c in range(groups):
        chosen = (index_ref[c : c + 1, :] == ids).astype(jnp.float32).astype(jnp.bfloat16)
        by_block_ref[c] = lax.dot_general(
            values_ref[c], chosen, (((1,), (1,)), ((), ())), preferred_element_type=jnp.float32
        )
    low = lax.broadcasted_iota(jnp.int32, (count, LANES), 1) < HALF
    for r in range(0, BLOCK, 2):
        rows = [
            by_block_ref[c, (r + odd) * cwidth : (r + odd + 1) * cwidth, :]
            for odd in (0, 1)
            for c in range(groups)
        ]
        pair = jnp.concatenate(rows, axis=0).T[:count]
        swapped = pltpu.roll(pair, HALF, 1)
        wide_ref[0, pl.ds(r, count, stride=BLOCK), :] = jnp.where(low, pair, 0.0)
        wide_ref[0, pl.ds(r + 1, count, stride=BLOCK), :] = jnp.where(low, swapped, 0.0)
        wide_ref[1, pl.ds(r, count, stride=BLOCK), :] = jnp.where(low, 0.0, swapped)
        wide_ref[1, pl.ds(r + 1, count, stride=BLOCK), :] = jnp.where(low, 0.0, pair)
    w_ref[...] = wide_ref[...].astype(jnp.bfloat16)


def build_out(index, values, first, count, after=()):
    groups, picks = index.shape
    values = values.transpose(0, 2, 3, 1).reshape(groups, -1, picks)
    rows = count * BLOCK
    return pl.pallas_call(
        functools.partial(build_out_kernel, count),
        out_shape=pltpu.VMEM((2, rows, LANES), jnp.bfloat16),
        in_specs=[IN_SMEM, IN_VMEM, IN_VMEM] + [ANY] * len(after),
        out_specs=IN_VMEM,
        scratch_shapes=[
            pltpu.VMEM((groups, values.shape[1], LANES), jnp.float32),
            pltpu.VMEM((2, rows, LANES), jnp.float32),
        ],
        compiler_params=PARAMS,
        cost_estimate=pl.CostEstimate(flops=10**9, bytes_accessed=values.size * 2, transcendentals=0),
    )(first[None].astype(jnp.int32), index, values, *after)


def project_kernel(tile, cuts, has_add, builds, after, *refs):
    refs = list(refs)
    roles_ref = refs.pop(0)
    x_hbm = refs.pop(0)
    if builds:
        index_hbm, values_hbm = refs.pop(0), refs.pop(0)
    else:
        w_ref = refs.pop(0)
    add_ref = refs.pop(0) if has_add else None
    refs = refs[after:]
    outs = [refs.pop(0) for _ in range(1 + max(cut[0] for cut in cuts))]
    if builds:
        w_ref = refs.pop(0)
    buf, sems = refs.pop(0), refs.pop(0)
    steps, filled = [], [0] * len(outs)
    for array, role, start, rows in cuts:
        for at in range(0, rows, tile):
            steps.append((array, role, start + at, filled[array]))
            filled[array] += tile

    def copies(i):
        _, role, row, _ = steps[i]
        base = pl.multiple_of(roles_ref[role] * LEN + roles_ref[4] * (LEN // 4) + row, tile)
        slot = i % SLOTS
        return [
            pltpu.make_async_copy(
                x_hbm.at[pl.ds(base + side * (LEN // 2), tile), :], buf.at[slot, side], sems.at[slot, side]
            )
            for side in (0, 1)
        ]

    if builds:
        index_ref, values_ref, build_sems, list_ref, acc_ref = refs
        loads = [
            pltpu.make_async_copy(index_hbm, index_ref, build_sems.at[0]),
            pltpu.make_async_copy(values_hbm, values_ref, build_sems.at[1]),
        ]
        for load in loads:
            load.start()
    for i in range(min(SLOTS, len(steps))):
        for copy in copies(i):
            copy.start()
    if builds:
        for load in loads:
            load.wait()
        build_in(roles_ref[5], index_ref, values_ref, w_ref, list_ref, acc_ref)
    for i, (array, _, _, at) in enumerate(steps):
        for copy in copies(i):
            copy.wait()
        slot = i % SLOTS
        value = jnp.dot(buf[slot, 0], w_ref[0], preferred_element_type=jnp.float32)
        value += jnp.dot(buf[slot, 1], w_ref[1], preferred_element_type=jnp.float32)
        if has_add:
            value += add_ref[i * tile : (i + 1) * tile, :]
        outs[array][at : at + tile, :] = value
        if i + SLOTS < len(steps):
            for copy in copies(i + SLOTS):
                copy.start()


def project(x, w, roles, add, tile, cuts, after=()):
    depth = x.shape[1]
    x = pltpu.with_memory_space_constraint(x, pltpu.HBM)
    rows = sum(cut[3] for cut in cuts)
    builds = isinstance(w, tuple)
    out_shape = [
        pltpu.VMEM((sum(cut[3] for cut in cuts if cut[0] == array), LANES), jnp.float32)
        for array in range(1 + max(cut[0] for cut in cuts))
    ]
    scratch = [
        pltpu.VMEM((SLOTS, 2, tile, depth), x.dtype),
        pltpu.SemaphoreType.DMA((SLOTS, 2)),
    ]
    if builds:
        index, values, count = w
        groups, picks = index.shape
        cwidth = values.shape[3]
        values = values.transpose(0, 1, 3, 2).reshape(groups * picks, cwidth, BLOCK)
        args = [roles, x, index, values]
        in_specs = [IN_SMEM, IN_HBM, IN_HBM, IN_HBM]
        out_shape.append(pltpu.VMEM((2, count * BLOCK, LANES), jnp.bfloat16))
        scratch += [
            pltpu.SMEM(index.shape, index.dtype),
            pltpu.VMEM(values.shape, values.dtype),
            pltpu.SemaphoreType.DMA((2,)),
            pltpu.SMEM((3, groups * picks), jnp.int32),
            pltpu.VMEM((count, groups * cwidth, LANES), jnp.float32),
        ]
    else:
        args = [roles, x, w]
        in_specs = [IN_SMEM, IN_HBM, IN_VMEM]
    if add is not None:
        args.append(add)
        in_specs.append(IN_VMEM)
    return pl.pallas_call(
        functools.partial(project_kernel, tile, cuts, add is not None, builds, len(after)),
        out_shape=out_shape,
        in_specs=in_specs + [ANY] * len(after),
        out_specs=[IN_VMEM] * len(out_shape),
        scratch_shapes=scratch,
        compiler_params=PARAMS,
        cost_estimate=pl.CostEstimate(
            flops=rows * depth * LANES, bytes_accessed=rows * depth, transcendentals=0
        ),
    )(*args, *after)


def contract(left, right):
    pair = lax.dot_general(
        left,
        right,
        (((0,), (0,)), ((), ())),
        precision=lax.Precision.HIGHEST,
        preferred_element_type=jnp.float32,
    )
    return pair[:HALF, :HALF] + pair[HALF:, HALF:]


def reduced_examples(tokens, up_grad, in_index, in_values, out_index, out_values):
    rank = lax.axis_index("store")
    core, x, z_low = rank % 2, (rank // 2) % 2, (rank // 4) % 2

    def swap(value, bit):
        return lax.ppermute(value, "store", [(i, i ^ bit) for i in range(16)])

    feat_blocks = tokens.shape[1] // BLOCK
    hidden_blocks = up_grad.shape[1] // BLOCK

    def roles(half):
        seqs = [1 - x, x, 3 - x, 2 + x]
        return jnp.stack([*seqs, half, rank * feat_blocks]).astype(jnp.int32)

    send, keep = roles(1 - core), roles(core)
    rows = LEN // 4
    half = rows // 2
    in_tile, out_tile = 256, 256

    def z_halves(value):
        halves = value.reshape(2, half, LANES)
        gone = lax.dynamic_index_in_dim(halves, 1 - z_low, 0, keepdims=False)
        kept = lax.dynamic_index_in_dim(halves, z_low, 0, keepdims=False)
        return kept + swap(gone, 4)

    def z_whole(kept):
        got = swap(kept, 4)
        return jnp.where(z_low == 0, jnp.stack([kept, got]), jnp.stack([got, kept])).reshape(-1, LANES)

    whole_a = [(0, 0, 0, rows), (1, 1, 0, rows)]
    whole_b = [(0, 2, 0, rows), (1, 3, 0, rows)]
    sent, in_w = project(
        tokens,
        (in_index, in_values, feat_blocks),
        send,
        None,
        in_tile,
        [(0, s, 0, rows) for s in range(4)],
    )
    got = swap(sent, 1)
    out_w = build_out(out_index, out_values, rank * hidden_blocks, hidden_blocks, after=(sent,))
    oa, ma, ob, mb = project(
        tokens, in_w, keep, got, in_tile, [(s, s, 0, rows) for s in range(4)], after=(out_w,)
    )
    in_a = ma + swap(oa, 2)
    in_b = mb + swap(ob, 2)
    (sent,) = project(
        up_grad, out_w, send, None, out_tile, [(0, 2, 0, rows), (0, 3, 0, rows)], after=(mb,)
    )
    got_b = swap(sent, 1)
    (sent,) = project(
        up_grad, out_w, send, None, out_tile, [(0, 0, 0, rows), (0, 1, 0, rows)], after=(in_a, sent)
    )
    got_a = swap(sent, 1)
    in_a = z_halves(in_a)
    ob, mb = project(up_grad, out_w, keep, got_b, out_tile, whole_b, after=(in_a, sent))
    in_a = in_a + swap(in_a, 8)
    in_b = z_halves(in_b)
    oa, ma = project(up_grad, out_w, keep, got_a, out_tile, whole_a, after=(mb, in_a))
    in_a = z_whole(in_a)
    out_b = z_halves(mb + swap(ob, 2))
    in_b = in_b + swap(in_b, 8)
    out_a = ma + swap(oa, 2)
    example = jnp.stack([contract(in_a, out_a), contract(in_b, out_b)]).reshape(-1, LANES)
    for bit in (1, 4, 8):
        example = example + swap(example, bit)
    other = swap(example, 2)
    example, other = example.reshape(2, HALF * HALF), other.reshape(2, HALF * HALF)
    first = jnp.where(x == 0, example, other)
    second = jnp.where(x == 0, other, example)
    return jnp.stack([first, second], axis=1).reshape(4, HALF * HALF) / LEN


def summed_examples(tokens, up_grad, in_index, in_values, out_index, out_values):
    rank = lax.axis_index("store")
    seqs = tokens.shape[0] // LEN
    feat_blocks = tokens.shape[1] // BLOCK
    hidden_blocks = up_grad.shape[1] // BLOCK
    out_proj = build_out(out_index, out_values, rank * hidden_blocks, hidden_blocks)
    rows = LEN // 4

    def packed(kind, w):
        made = []
        for s in range(0, seqs, 2):
            for h in (0, 1):
                roles = jnp.stack([s, s + 1, s, s, h, rank * feat_blocks]).astype(jnp.int32)
                first, second, *rest = project(
                    kind, w, roles, None, 256, [(0, 0, 0, rows), (1, 1, 0, rows)]
                )
                if rest:
                    w = rest[0]
                made.append(jnp.stack([first, second]))
        return jnp.concatenate(made)

    ins, outs = lax.psum(
        (packed(tokens, (in_index, in_values, feat_blocks)), packed(up_grad, out_proj)), "store"
    )
    pair = jnp.einsum("slp,slq->spq", ins, outs, precision=lax.Precision.HIGHEST)
    pair = pair[:, :HALF, :HALF] + pair[:, HALF:, HALF:]
    pair = pair.reshape(seqs // 2, 2, 2, HALF * HALF).sum(1) / LEN
    return pair.reshape(seqs, HALF * HALF)


def on_device(size, tokens, up_grad, in_index, in_values, out_index, out_values, stored):
    whole = reduced_examples if size == 16 and tokens.shape[0] == 4 * LEN else summed_examples
    example = whole(tokens, up_grad, in_index, in_values, out_index, out_values)
    return lax.dot_general(
        example.astype(jnp.bfloat16),
        stored,
        (((1,), (1,)), ((), ())),
        preferred_element_type=jnp.float32,
    )


def solution(mesh):
    return jax.shard_map(
        functools.partial(on_device, mesh.shape["store"]),
        mesh=mesh,
        in_specs=(
            P("groups", "store"),
            P("groups", "store"),
            P(),
            P(),
            P(),
            P(),
            P(("groups", "store"), None),
        ),
        out_specs=P("groups", "store"),
        check_vma=False,
    )
```

time: 247 us -> 122 us (0.49)
  waiting for transfers between devices: 173 us -> 36 us
  Pallas kernels: 0 us -> 52.7 us
  matrix products: 51 us -> 3.91 us
  starting transfers between devices: 0.01 us -> 16.7 us
  between operations: 13.5 us -> 0.27 us
  other arithmetic: 0.01 us -> 4.8 us
    psum x1 -> x0, waiting for transfers between devices: 173 us -> none  [on_device(): inputs, outputs = lax.psum((in_part, out_part), 'store')]
    pallas_call x0 -> x7, Pallas kernels: none -> 52.7 us  [the longest x6 51.1 us: project(): pl.pallas_call(functools.partial(project_kernel, tile, cuts, add is not N...]
    dot_general x6 -> x3, matrix products: 51 us -> 3.91 us  [the longest x2 2.66 us: contract(): lax.dot_general(left, right, (((0,), (0,)), ((), ())), precision=lax.Prec...]
    ppermute x0 -> x17, waiting for transfers between devices: none -> 36 us  [swap(): return lax.ppermute(value, 'store', [(i, i ^ bit) for i in range(16)])]
    ppermute x0 -> x17, starting transfers between devices: none -> 16.7 us  [swap(): return lax.ppermute(value, 'store', [(i, i ^ bit) for i in range(16)])]
    reshape x1, local copies, waits for them, and re-layouts: 7.69 us -> 0.07 us  [reduced_examples(): jnp.stack([contract(in_a, out_a), contract(in_b, out_b)]).reshape(-1, LANES)]
    unnamed x4 -> x26, local copies, waits for them, and re-layouts: 0.01 us -> 5.56 us
    add x2 -> x9, other arithmetic: 0.01 us -> 3.49 us  [the longest x1 1.25 us: reduced_examples(): in_a = ma + swap(oa, 2)]
  transfers between devices with their start and end apart: 1 -> 17, of which waited for: 1 -> 10; matrix products, arithmetic and copies ran while one was open for 0% -> 6% of each run, Pallas kernels for 0% -> 28%
where the time goes in v1:
time: 122 us
  Pallas kernels  52.7 us (43%)
  waiting for transfers between devices  36 us (30%)
  starting transfers between devices  16.7 us (14%)
  local copies, waits for them, and re-layouts  7.3 us (6%)
  other arithmetic  4.8 us (4%)
  matrix products  3.91 us (3%)
    pallas_call x6, Pallas kernels, project(): pl.pallas_call(functools.partial(project_kernel, tile, cuts, add is not N...  51.1 us
    ppermute x17, waiting for transfers between devices, swap(): return lax.ppermute(value, 'store', [(i, i ^ bit) for i in range(16)])  36 us
    ppermute x17, starting transfers between devices, swap(): return lax.ppermute(value, 'store', [(i, i ^ bit) for i in range(16)])  16.7 us
    unnamed x26, local copies, waits for them, and re-layouts  5.56 us
    dot_general x2, matrix products, contract(): lax.dot_general(left, right, (((0,), (0,)), ((), ())), precision=lax.Prec...  2.66 us
  transfers between devices with their start and end apart: 17, of which 10 were waited for; matrix products, arithmetic and copies ran while one was open for 6% of the time, Pallas kernels for 28%

profile of v1, /device:TPU:0, one launch (start us, length us, event | category | flops | bytes accessed | tf_op | source)
XLA Modules:
  0.0 121.7 jit_solution(179700451154039265)
XLA Ops:
  2.0 10.0 %shard_map.73 = (f32[4096,128]{1,0:T(8,128)}, bf16[2,512,128]{2,1,0:T(8,128)(2,1)S(1)}) custom-call(s32[6]{0:T(128)S(1)} %stack.68.refs_0_, bf16[16384,512]{1,0:T(8,128)(2,1)} %refs_1_.7, s32[8,32]{1,0:T(8,128)S(1)} %copy-done.7, bf16[256,8,32]{2,1,0:T(8,128)(2,1)S(1)} %bitcast.45), custom_call_target="tpu_custom_call" | custom-call | flops 268435456 | bytes 2097152 | tf_op jit(solution)/shard_map/pallas_call | solution.py:193
  13.6 1.6 %shard_map.74.refs_4_.refs_2_ = bf16[2,1792,128]{2,1,0:T(8,128)(2,1)S(1)} custom-call(s32[1]{0:T(128)} %bitcast.9.first_ref, s32[8,112]{1,0:T(8,128)S(1)} %copy-done.9, bf16[8,256,112]{2,1,0:T(8,128)(2,1)S(1)} %bitcast.46, f32[4096,128]{1,0:T(8,128)} %get-tuple-element.16.rest_0_), custom_call_target="tpu_custom_call" | custom-call | flops 1000000000 | bytes 458752 | tf_op jit(solution)/shard_map/pallas_call | solution.py:85
  15.2 1.4 %collective-permute-done.refs_3_ = f32[4096,128]{1,0:T(8,128)} collective-permute-done((f32[4096,128]{1,0:T(8,128)}, f32[4096,128]{1,0:T(8,128)}, u32[]{:S(2)}, u32[]{:S(2)}) %collective-permute-start) | collective-permute-done | bytes 2097184 | tf_op jit(solution)/shard_map/ppermute | solution.py:222
  16.6 8.5 %shard_map.75 = (f32[1024,128]{1,0:T(8,128)}, f32[1024,128]{1,0:T(8,128)S(1)}, f32[1024,128]{1,0:T(8,128)}, f32[1024,128]{1,0:T(8,128)S(1)}) custom-call(s32[6]{0:T(128)S(1)} %stack.66.refs_0_, bf16[16384,512]{1,0:T(8,128)(2,1)} %refs_1_.7, bf16[2,512,128]{2,1,0:T(8,128)(2,1)S(1)} %get-tuple-element.15.refs_2_, f32[4096,128]{1,0:T(8,128)} %collective-permute-done.refs_3_, ...), custom_call_target="tpu_custom_call" | custom-call | flops 268435456 | bytes 2097152 | tf_op jit(solution)/shard_map/pallas_call | solution.py:193
  25.1 2.8 %collective-permute-start.1 = (f32[1024,128]{1,0:T(8,128)}, f32[1024,128]{1,0:T(8,128)S(1)}, u32[]{:S(2)}, u32[]{:S(2)}) collective-permute-start(f32[1024,128]{1,0:T(8,128)} %get-tuple-element.18), channel_id=1, source_target_pairs={{0,2},{1,3},{2,0},{3,1},{4,6},{5,7},{6,4},{7,5},{8,10},{9,11},{10,... | collective-permute-start | bytes 1572872 | tf_op jit(solution)/shard_map/ppermute | solution.py:222
  28.0 8.4 %shard_map.76.refs_4_ = f32[2048,128]{1,0:T(8,128)} custom-call(s32[6]{0:T(128)S(1)} %stack.68.refs_0_, bf16[16384,1792]{1,0:T(8,128)(2,1)} %refs_1_.11, bf16[2,1792,128]{2,1,0:T(8,128)(2,1)S(1)} %shard_map.74.refs_4_.refs_2_, f32[1024,128]{1,0:T(8,128)S(1)} %get-tuple-element.19.refs_3_), custom_call_target="tpu_custom_call" | custom-call | flops 469762048 | bytes 3670016 | tf_op jit(solution)/shard_map/pallas_call | solution.py:193
  36.6 4.3 %collective-permute-done.1 = f32[1024,128]{1,0:T(8,128)S(1)} collective-permute-done((f32[1024,128]{1,0:T(8,128)}, f32[1024,128]{1,0:T(8,128)S(1)}, u32[]{:S(2)}, u32[]{:S(2)}) %collective-permute-start.1) | collective-permute-done | bytes 524320 | tf_op jit(solution)/shard_map/ppermute | solution.py:222
  43.7 2.2 %collective-permute-start.2 = (f32[512,128]{1,0:T(8,128)}, f32[512,128]{1,0:T(8,128)}, u32[]{:S(2)}, u32[]{:S(2)}) collective-permute-start(f32[512,128]{1,0:T(8,128)} %dynamic-slice_bitcast_fusion.2), channel_id=1, source_target_pairs={{0,4},{1,5},{2,6},{3,7},{4,0},{5,1},{6,2},{7,3},{8,12},{9,13},{10,... | collective-permute-start | bytes 786440 | tf_op jit(solution)/shard_map/ppermute | solution.py:222
  45.8 8.2 %shard_map.77.refs_5_ = f32[2048,128]{1,0:T(8,128)} custom-call(s32[6]{0:T(128)S(1)} %stack.68.refs_0_, bf16[16384,1792]{1,0:T(8,128)(2,1)} %refs_1_.11, bf16[2,1792,128]{2,1,0:T(8,128)(2,1)S(1)} %shard_map.74.refs_4_.refs_2_, f32[1024,128]{1,0:T(8,128)S(1)} %add.74.refs_3_, f32[2048,128]{1,0:T(8,128)} %shard_map.76.refs_4_), custom_call_target="tpu_custom_call" | custom-call | flops 469762048 | bytes 3670016 | tf_op jit(solution)/shard_map/pallas_call | solution.py:193
  56.2 2.6 %collective-permute-start.3 = (f32[512,128]{1,0:T(8,128)S(1)}, f32[512,128]{1,0:T(8,128)S(1)}, u32[]{:S(2)}, u32[]{:S(2)}) collective-permute-start(f32[512,128]{1,0:T(8,128)S(1)} %bitcast_add_fusion.3.refs_4_), channel_id=1, source_target_pairs={{0,8},{1,9},{2,10},{3,11},{4,12},{5,13},{6,14},{7,15},{8,0},{9,1},... | collective-permute-start | bytes 786440 | tf_op jit(solution)/shard_map/ppermute | solution.py:222
  58.8 7.9 %shard_map.78 = (f32[1024,128]{1,0:T(8,128)S(1)}, f32[1024,128]{1,0:T(8,128)S(1)}) custom-call(s32[6]{0:T(128)S(1)} %stack.66.refs_0_, bf16[16384,1792]{1,0:T(8,128)(2,1)} %refs_1_.11, bf16[2,1792,128]{2,1,0:T(8,128)(2,1)S(1)} %shard_map.74.refs_4_.refs_2_, f32[2048,128]{1,0:T(8,128)} %collective-permute-done.6.refs_3_, ...), custom_call_target="tpu_custom_call" | custom-call | flops 469762048 | bytes 3670016 | tf_op jit(solution)/shard_map/pallas_call | solution.py:193
  66.8 1.6 %collective-permute-start.11 = (f32[1024,128]{1,0:T(8,128)S(1)}, f32[1024,128]{1,0:T(8,128)S(1)}, u32[]{:S(2)}, u32[]{:S(2)}) collective-permute-start(f32[1024,128]{1,0:T(8,128)S(1)} %get-tuple-element.24), channel_id=1, source_target_pairs={{0,2},{1,3},{2,0},{3,1},{4,6},{5,7},{6,4},{7,5},{8,10},{9,11},{10,... | collective-permute-start | bytes 1572872 | tf_op jit(solution)/shard_map/ppermute | solution.py:222
  68.9 2.5 %collective-permute-done.3 = f32[512,128]{1,0:T(8,128)S(1)} collective-permute-done((f32[512,128]{1,0:T(8,128)S(1)}, f32[512,128]{1,0:T(8,128)S(1)}, u32[]{:S(2)}, u32[]{:S(2)}) %collective-permute-start.3) | collective-permute-done | bytes 262176 | tf_op jit(solution)/shard_map/ppermute | solution.py:222
  71.4 6.2 %collective-permute-done.9 = f32[512,128]{1,0:T(8,128)S(1)} collective-permute-done((f32[512,128]{1,0:T(8,128)S(1)}, f32[512,128]{1,0:T(8,128)S(1)}, u32[]{:S(2)}, u32[]{:S(2)}) %collective-permute-start.9) | collective-permute-done | bytes 262176 | tf_op jit(solution)/shard_map/ppermute | solution.py:222
  78.0 2.8 %collective-permute-done.11 = f32[1024,128]{1,0:T(8,128)S(1)} collective-permute-done((f32[1024,128]{1,0:T(8,128)S(1)}, f32[1024,128]{1,0:T(8,128)S(1)}, u32[]{:S(2)}, u32[]{:S(2)}) %collective-permute-start.11) | collective-permute-done | bytes 524320 | tf_op jit(solution)/shard_map/ppermute | solution.py:222
  83.9 8.2 %shard_map.79 = (f32[1024,128]{1,0:T(8,128)S(1)}, f32[1024,128]{1,0:T(8,128)S(1)}) custom-call(s32[6]{0:T(128)S(1)} %stack.66.refs_0_, bf16[16384,1792]{1,0:T(8,128)(2,1)} %refs_1_.11, bf16[2,1792,128]{2,1,0:T(8,128)(2,1)S(1)} %shard_map.74.refs_4_.refs_2_, f32[2048,128]{1,0:T(8,128)} %collective-permute-done.5.refs_3_, f32[1024,128]{1,0:T(8,128)S(1)} %copy-done.4, ...), custom_call_target="tpu_custom_call" | custom-call | flops 469762048 | bytes 3670016 | tf_op jit(solution)/shard_map/pallas_call | solution.py:193
  92.1 1.6 %collective-permute-start.7 = (f32[1024,128]{1,0:T(8,128)S(1)}, f32[1024,128]{1,0:T(8,128)S(1)}, u32[]{:S(2)}, u32[]{:S(2)}) collective-permute-start(f32[1024,128]{1,0:T(8,128)S(1)} %get-tuple-element.22), channel_id=1, source_target_pairs={{0,2},{1,3},{2,0},{3,1},{4,6},{5,7},{6,4},{7,5},{8,10},{9,11},{10,... | collective-permute-start | bytes 1572872 | tf_op jit(solution)/shard_map/ppermute | solution.py:222
  94.8 1.6 %fusion.2 = f32[128,128]{1,0:T(8,128)S(1)} fusion(f32[512,128]{1,0:T(8,128)} %collective-permute-done.12, f32[2,512,128]{2,1,0:T(8,128)S(1)} %bitcast.50, s32[]{:T(128)S(6)} %select_n.84, f32[512,128]{1,0:T(8,128)S(1)} %bitcast_add_fusion.2, f32[512,128]{1,0:T(8,128)} %collective-permute-done.10), kind=kOutput, calls=%fused_computation.4 | convolution fusion | flops 100794368 | bytes 1114116 | tf_op jit(solution)/shard_map/dot_general | solution.py:207
  96.5 8.7 %collective-permute-done.7 = f32[1024,128]{1,0:T(8,128)S(1)} collective-permute-done((f32[1024,128]{1,0:T(8,128)S(1)}, f32[1024,128]{1,0:T(8,128)S(1)}, u32[]{:S(2)}, u32[]{:S(2)}) %collective-permute-start.7) | collective-permute-done | bytes 524320 | tf_op jit(solution)/shard_map/ppermute | solution.py:222
  107.6 1.6 %collective-permute-start.14 = (f32[64,128]{1,0:T(8,128)S(1)}, f32[64,128]{1,0:T(8,128)S(1)}, u32[]{:S(2)}, u32[]{:S(2)}) collective-permute-start(f32[64,128]{1,0:T(8,128)S(1)} %add.87), channel_id=1, source_target_pairs={{0,4},{1,5},{2,6},{3,7},{4,0},{5,1},{6,2},{7,3},{8,12},{9,13},{10,... | collective-permute-start | bytes 98312 | tf_op jit(solution)/shard_map/ppermute | solution.py:222
  109.2 2.3 %collective-permute-done.14 = f32[64,128]{1,0:T(8,128)S(1)} collective-permute-done((f32[64,128]{1,0:T(8,128)S(1)}, f32[64,128]{1,0:T(8,128)S(1)}, u32[]{:S(2)}, u32[]{:S(2)}) %collective-permute-start.14) | collective-permute-done | bytes 32800 | tf_op jit(solution)/shard_map/ppermute | solution.py:222
  112.2 4.2 %collective-permute-done.15 = f32[64,128]{1,0:T(8,128)S(1)} collective-permute-done((f32[64,128]{1,0:T(8,128)S(1)}, f32[64,128]{1,0:T(8,128)S(1)}, u32[]{:S(2)}, u32[]{:S(2)}) %collective-permute-start.15) | collective-permute-done | bytes 32800 | tf_op jit(solution)/shard_map/ppermute | solution.py:222
  116.4 1.5 %collective-permute-start.16 = (f32[64,128]{1,0:T(8,128)S(1)}, f32[64,128]{1,0:T(8,128)S(1)}, u32[]{:S(2)}, u32[]{:S(2)}) collective-permute-start(f32[64,128]{1,0:T(8,128)S(1)} %add.89), channel_id=1, source_target_pairs={{0,2},{1,3},{2,0},{3,1},{4,6},{5,7},{6,4},{7,5},{8,10},{9,11},{10,... | collective-permute-start | bytes 98312 | tf_op jit(solution)/shard_map/ppermute | solution.py:222
  117.9 2.4 %collective-permute-done.16 = f32[64,128]{1,0:T(8,128)S(1)} collective-permute-done((f32[64,128]{1,0:T(8,128)S(1)}, f32[64,128]{1,0:T(8,128)S(1)}, u32[]{:S(2)}, u32[]{:S(2)}) %collective-permute-start.16) | collective-permute-done | bytes 32800 | tf_op jit(solution)/shard_map/ppermute | solution.py:222
  (68 shorter events, 18.5 us)
Async XLA Ops:
  0.0 120.4 %copy-start = (bf16[256,4096]{1,0:T(8,128)(2,1)S(1)}, bf16[256,4096]{1,0:T(8,128)(2,1)}, u32[]{:S(2)}) copy-start(bf16[256,4096]{1,0:T(8,128)(2,1)} %param.13) | copy-start | bytes 6291460
  2.0 10.6 %copy-start.9 = (s32[8,112]{1,0:T(8,128)S(1)}, s32[8,112]{1,0:T(8,128)}, u32[]{:S(2)}) copy-start(s32[8,112]{1,0:T(8,128)} %index_ref.1) | copy-start | bytes 10756
  11.9 4.7 %collective-permute-start = (f32[4096,128]{1,0:T(8,128)}, f32[4096,128]{1,0:T(8,128)}, u32[]{:S(2)}, u32[]{:S(2)}) collective-permute-start(f32[4096,128]{1,0:T(8,128)} %get-tuple-element.16.rest_0_), channel_id=1, source_target_pairs={{0,1},{1,0},{2,3},{3,2},{4,5},{5,4},{6,7},{7,6},{8,9},{9,8},{10,11... | collective-permute-start | bytes 6291464 | tf_op jit(solution)/shard_map/ppermute | solution.py:222
  25.1 11.2 %copy-start.1 = (f32[1024,128]{1,0:T(8,128)}, f32[1024,128]{1,0:T(8,128)S(1)}, u32[]{:S(2)}) copy-start(f32[1024,128]{1,0:T(8,128)S(1)} %get-tuple-element.19.refs_3_) | copy-start | bytes 1572868
  25.1 11.2 %copy-start.6 = (f32[1024,128]{1,0:T(8,128)}, f32[1024,128]{1,0:T(8,128)S(1)}, u32[]{:S(2)}) copy-start(f32[1024,128]{1,0:T(8,128)S(1)} %get-tuple-element.17) | copy-start | bytes 1572868
  25.1 15.7 %collective-permute-start.1 = (f32[1024,128]{1,0:T(8,128)}, f32[1024,128]{1,0:T(8,128)S(1)}, u32[]{:S(2)}, u32[]{:S(2)}) collective-permute-start(f32[1024,128]{1,0:T(8,128)} %get-tuple-element.18), channel_id=1, source_target_pairs={{0,2},{1,3},{2,0},{3,1},{4,6},{5,7},{6,4},{7,5},{8,10},{9,11},{10,... | collective-permute-start | bytes 1572872 | tf_op jit(solution)/shard_map/ppermute | solution.py:222
  36.4 22.5 %collective-permute-start.6 = (f32[2048,128]{1,0:T(8,128)}, f32[2048,128]{1,0:T(8,128)}, u32[]{:S(2)}, u32[]{:S(2)}) collective-permute-start(f32[2048,128]{1,0:T(8,128)} %shard_map.76.refs_4_), channel_id=1, source_target_pairs={{0,1},{1,0},{2,3},{3,2},{4,5},{5,4},{6,7},{7,6},{8,9},{9,8},{10,11... | collective-permute-start | bytes 3145736 | tf_op jit(solution)/shard_map/ppermute | solution.py:222
  36.5 17.6 %collective-permute-start.8 = (f32[1024,128]{1,0:T(8,128)}, f32[1024,128]{1,0:T(8,128)}, u32[]{:S(2)}, u32[]{:S(2)}) collective-permute-start(f32[1024,128]{1,0:T(8,128)} %get-tuple-element.23), channel_id=1, source_target_pairs={{0,2},{1,3},{2,0},{3,1},{4,6},{5,7},{6,4},{7,5},{8,10},{9,11},{10,... | collective-permute-start | bytes 1572872 | tf_op jit(solution)/shard_map/ppermute | solution.py:222
  43.7 11.5 %collective-permute-start.2 = (f32[512,128]{1,0:T(8,128)}, f32[512,128]{1,0:T(8,128)}, u32[]{:S(2)}, u32[]{:S(2)}) collective-permute-start(f32[512,128]{1,0:T(8,128)} %dynamic-slice_bitcast_fusion.2), channel_id=1, source_target_pairs={{0,4},{1,5},{2,6},{3,7},{4,0},{5,1},{6,2},{7,3},{8,12},{9,13},{10,... | collective-permute-start | bytes 786440 | tf_op jit(solution)/shard_map/ppermute | solution.py:222
  45.8 8.3 %copy-start.2 = (f32[1024,128]{1,0:T(8,128)S(1)}, f32[1024,128]{1,0:T(8,128)}, u32[]{:S(2)}) copy-start(f32[1024,128]{1,0:T(8,128)} %copy-done.1) | copy-start | bytes 1572868
  54.0 28.9 %collective-permute-start.5 = (f32[2048,128]{1,0:T(8,128)}, f32[2048,128]{1,0:T(8,128)}, u32[]{:S(2)}, u32[]{:S(2)}) collective-permute-start(f32[2048,128]{1,0:T(8,128)} %shard_map.77.refs_5_), channel_id=1, source_target_pairs={{0,1},{1,0},{2,3},{3,2},{4,5},{5,4},{6,7},{7,6},{8,9},{9,8},{10,11... | collective-permute-start | bytes 3145736 | tf_op jit(solution)/shard_map/ppermute | solution.py:222
  56.2 15.1 %collective-permute-start.3 = (f32[512,128]{1,0:T(8,128)S(1)}, f32[512,128]{1,0:T(8,128)S(1)}, u32[]{:S(2)}, u32[]{:S(2)}) collective-permute-start(f32[512,128]{1,0:T(8,128)S(1)} %bitcast_add_fusion.3.refs_4_), channel_id=1, source_target_pairs={{0,8},{1,9},{2,10},{3,11},{4,12},{5,13},{6,14},{7,15},{8,0},{9,1},... | collective-permute-start | bytes 786440 | tf_op jit(solution)/shard_map/ppermute | solution.py:222
  66.7 15.7 %copy-start.3 = (f32[1024,128]{1,0:T(8,128)}, f32[1024,128]{1,0:T(8,128)S(1)}, u32[]{:S(2)}) copy-start(f32[1024,128]{1,0:T(8,128)S(1)} %get-tuple-element.20.refs_4_) | copy-start | bytes 1572868
  66.8 14.1 %collective-permute-start.11 = (f32[1024,128]{1,0:T(8,128)S(1)}, f32[1024,128]{1,0:T(8,128)S(1)}, u32[]{:S(2)}, u32[]{:S(2)}) collective-permute-start(f32[1024,128]{1,0:T(8,128)S(1)} %get-tuple-element.24), channel_id=1, source_target_pairs={{0,2},{1,3},{2,0},{3,1},{4,6},{5,7},{6,4},{7,5},{8,10},{9,11},{10,... | collective-permute-start | bytes 1572872 | tf_op jit(solution)/shard_map/ppermute | solution.py:222
  68.4 9.3 %collective-permute-start.9 = (f32[512,128]{1,0:T(8,128)S(1)}, f32[512,128]{1,0:T(8,128)S(1)}, u32[]{:S(2)}, u32[]{:S(2)}) collective-permute-start(f32[512,128]{1,0:T(8,128)S(1)} %dynamic-slice_bitcast_fusion.1), channel_id=1, source_target_pairs={{0,4},{1,5},{2,6},{3,7},{4,0},{5,1},{6,2},{7,3},{8,12},{9,13},{10,... | collective-permute-start | bytes 786440 | tf_op jit(solution)/shard_map/ppermute | solution.py:222
  71.4 22.3 %collective-permute-start.4 = (f32[512,128]{1,0:T(8,128)S(1)}, f32[512,128]{1,0:T(8,128)}, u32[]{:S(2)}, u32[]{:S(2)}) collective-permute-start(f32[512,128]{1,0:T(8,128)S(1)} %add.78.refs_5_), channel_id=1, source_target_pairs={{0,4},{1,5},{2,6},{3,7},{4,0},{5,1},{6,2},{7,3},{8,12},{9,13},{10,... | collective-permute-start | bytes 786440 | tf_op jit(solution)/shard_map/ppermute | solution.py:222
  77.6 17.1 %collective-permute-start.10 = (f32[512,128]{1,0:T(8,128)S(1)}, f32[512,128]{1,0:T(8,128)}, u32[]{:S(2)}, u32[]{:S(2)}) collective-permute-start(f32[512,128]{1,0:T(8,128)S(1)} %bitcast_add_fusion.2), channel_id=1, source_target_pairs={{0,8},{1,9},{2,10},{3,11},{4,12},{5,13},{6,14},{7,15},{8,0},{9,1},... | collective-permute-start | bytes 786440 | tf_op jit(solution)/shard_map/ppermute | solution.py:222
  82.5 12.3 %collective-permute-start.12 = (f32[512,128]{1,0:T(8,128)}, f32[512,128]{1,0:T(8,128)}, u32[]{:S(2)}, u32[]{:S(2)}) collective-permute-start(f32[512,128]{1,0:T(8,128)} %dynamic-slice_bitcast_fusion), channel_id=1, source_target_pairs={{0,4},{1,5},{2,6},{3,7},{4,0},{5,1},{6,2},{7,3},{8,12},{9,13},{10,... | collective-permute-start | bytes 786440 | tf_op jit(solution)/shard_map/ppermute | solution.py:222
  83.9 10.9 %copy-start.11 = (f32[1024,128]{1,0:T(8,128)S(1)}, f32[1024,128]{1,0:T(8,128)}, u32[]{:S(2)}) copy-start(f32[1024,128]{1,0:T(8,128)} %copy-done.10) | copy-start | bytes 1572868
  92.1 13.1 %collective-permute-start.7 = (f32[1024,128]{1,0:T(8,128)S(1)}, f32[1024,128]{1,0:T(8,128)S(1)}, u32[]{:S(2)}, u32[]{:S(2)}) collective-permute-start(f32[1024,128]{1,0:T(8,128)S(1)} %get-tuple-element.22), channel_id=1, source_target_pairs={{0,2},{1,3},{2,0},{3,1},{4,6},{5,7},{6,4},{7,5},{8,10},{9,11},{10,... | collective-permute-start | bytes 1572872 | tf_op jit(solution)/shard_map/ppermute | solution.py:222
  106.4 1.2 %collective-permute-start.13 = (f32[64,128]{1,0:T(8,128)S(1)}, f32[64,128]{1,0:T(8,128)S(1)}, u32[]{:S(2)}, u32[]{:S(2)}) collective-permute-start(f32[64,128]{1,0:T(8,128)S(1)} %reshape.72), channel_id=1, source_target_pairs={{0,1},{1,0},{2,3},{3,2},{4,5},{5,4},{6,7},{7,6},{8,9},{9,8},{10,11... | collective-permute-start | bytes 98312 | tf_op jit(solution)/shard_map/ppermute | solution.py:222
  107.6 3.9 %collective-permute-start.14 = (f32[64,128]{1,0:T(8,128)S(1)}, f32[64,128]{1,0:T(8,128)S(1)}, u32[]{:S(2)}, u32[]{:S(2)}) collective-permute-start(f32[64,128]{1,0:T(8,128)S(1)} %add.87), channel_id=1, source_target_pairs={{0,4},{1,5},{2,6},{3,7},{4,0},{5,1},{6,2},{7,3},{8,12},{9,13},{10,... | collective-permute-start | bytes 98312 | tf_op jit(solution)/shard_map/ppermute | solution.py:222
  111.6 4.8 %collective-permute-start.15 = (f32[64,128]{1,0:T(8,128)S(1)}, f32[64,128]{1,0:T(8,128)S(1)}, u32[]{:S(2)}, u32[]{:S(2)}) collective-permute-start(f32[64,128]{1,0:T(8,128)S(1)} %add.88), channel_id=1, source_target_pairs={{0,8},{1,9},{2,10},{3,11},{4,12},{5,13},{6,14},{7,15},{8,0},{9,1},... | collective-permute-start | bytes 98312 | tf_op jit(solution)/shard_map/ppermute | solution.py:222
  116.4 3.9 %collective-permute-start.16 = (f32[64,128]{1,0:T(8,128)S(1)}, f32[64,128]{1,0:T(8,128)S(1)}, u32[]{:S(2)}, u32[]{:S(2)}) collective-permute-start(f32[64,128]{1,0:T(8,128)S(1)} %add.89), channel_id=1, source_target_pairs={{0,2},{1,3},{2,0},{3,1},{4,6},{5,7},{6,4},{7,5},{8,10},{9,11},{10,... | collective-permute-start | bytes 98312 | tf_op jit(solution)/shard_map/ppermute | solution.py:222
  (6 other events, 5.5 us)

commit v2 on v1

--- a/solution.py
+++ b/solution.py
@@ -96,7 +96,7 @@
     )(first[None].astype(jnp.int32), index, values, *after)
 
 
-def project_kernel(tile, cuts, has_add, builds, after, *refs):
+def project_kernel(tile, cuts, has_add, builds, after, through, *refs):
     refs = list(refs)
     roles_ref = refs.pop(0)
     x_hbm = refs.pop(0)
@@ -105,10 +105,11 @@
     else:
         w_ref = refs.pop(0)
     add_ref = refs.pop(0) if has_add else None
-    refs = refs[after:]
+    refs = refs[after + through :]
     outs = [refs.pop(0) for _ in range(1 + max(cut[0] for cut in cuts))]
     if builds:
         w_ref = refs.pop(0)
+    refs = refs[through:]
     buf, sems = refs.pop(0), refs.pop(0)
     steps, filled = [], [0] * len(outs)
     for array, role, start, rows in cuts:
@@ -156,7 +157,7 @@
                 copy.start()
 
 
-def project(x, w, roles, add, tile, cuts, after=()):
+def project(x, w, roles, add, tile, cuts, after=(), through=()):
     depth = x.shape[1]
     x = pltpu.with_memory_space_constraint(x, pltpu.HBM)
     rows = sum(cut[3] for cut in cuts)
@@ -174,6 +175,8 @@
         groups, picks = index.shape
         cwidth = values.shape[3]
         values = values.transpose(0, 1, 3, 2).reshape(groups * picks, cwidth, BLOCK)
+        index = pltpu.with_memory_space_constraint(index, pltpu.HBM)
+        values = pltpu.with_memory_space_constraint(values, pltpu.HBM)
         args = [roles, x, index, values]
         in_specs = [IN_SMEM, IN_HBM, IN_HBM, IN_HBM]
         out_shape.append(pltpu.VMEM((2, count * BLOCK, LANES), jnp.bfloat16))
@@ -191,16 +194,31 @@
         args.append(add)
         in_specs.append(IN_VMEM)
     return pl.pallas_call(
-        functools.partial(project_kernel, tile, cuts, add is not None, builds, len(after)),
-        out_shape=out_shape,
-        in_specs=in_specs + [ANY] * len(after),
-        out_specs=[IN_VMEM] * len(out_shape),
+        functools.partial(project_kernel, tile, cuts, add is not None, builds, len(after), len(through)),
+        out_shape=out_shape + [jax.ShapeDtypeStruct(t.shape, t.dtype) for t in through],
+        in_specs=in_specs + [ANY] * (len(after) + len(through)),
+        out_specs=[IN_VMEM] * len(out_shape) + [ANY] * len(through),
+        input_output_aliases={
+            len(args) + len(after) + i: len(out_shape) + i for i in range(len(through))
+        },
         scratch_shapes=scratch,
         compiler_params=PARAMS,
         cost_estimate=pl.CostEstimate(
             flops=rows * depth * LANES, bytes_accessed=rows * depth, transcendentals=0
         ),
-    )(*args, *after)
+    )(*args, *after, *through)
+
+
+def held(values, after):
+    count = len(values)
+    return pl.pallas_call(
+        lambda *refs: None,
+        out_shape=[jax.ShapeDtypeStruct(v.shape, v.dtype) for v in values],
+        in_specs=[ANY] * (count + len(after)),
+        out_specs=[ANY] * count,
+        input_output_aliases={i: i for i in range(count)},
+        cost_estimate=pl.CostEstimate(flops=0, bytes_accessed=0, transcendentals=0),
+    )(*values, *after)
 
 
 def contract(left, right):
@@ -237,7 +255,7 @@
         halves = value.reshape(2, half, LANES)
         gone = lax.dynamic_index_in_dim(halves, 1 - z_low, 0, keepdims=False)
         kept = lax.dynamic_index_in_dim(halves, z_low, 0, keepdims=False)
-        return kept + swap(gone, 4)
+        return kept, swap(gone, 4)
 
     def z_whole(kept):
         got = swap(kept, 4)
@@ -255,28 +273,43 @@
     )
     got = swap(sent, 1)
     out_w = build_out(out_index, out_values, rank * hidden_blocks, hidden_blocks, after=(sent,))
-    oa, ma, ob, mb = project(
+    oa, in_a, ob, in_b = project(
         tokens, in_w, keep, got, in_tile, [(s, s, 0, rows) for s in range(4)], after=(out_w,)
     )
-    in_a = ma + swap(oa, 2)
-    in_b = mb + swap(ob, 2)
-    (sent,) = project(
-        up_grad, out_w, send, None, out_tile, [(0, 2, 0, rows), (0, 3, 0, rows)], after=(mb,)
-    )
-    got_b = swap(sent, 1)
-    (sent,) = project(
-        up_grad, out_w, send, None, out_tile, [(0, 0, 0, rows), (0, 1, 0, rows)], after=(in_a, sent)
-    )
-    got_a = swap(sent, 1)
-    in_a = z_halves(in_a)
-    ob, mb = project(up_grad, out_w, keep, got_b, out_tile, whole_b, after=(in_a, sent))
-    in_a = in_a + swap(in_a, 8)
-    in_b = z_halves(in_b)
-    oa, ma = project(up_grad, out_w, keep, got_a, out_tile, whole_a, after=(mb, in_a))
+    got_in_a, got_in_b = swap(oa, 2), swap(ob, 2)
+    sent_b, sent_a, in_a = project(
+        up_grad,
+        out_w,
+        send,
+        None,
+        out_tile,
+        [(0, 2, 0, rows), (0, 3, 0, rows), (1, 0, 0, rows), (1, 1, 0, rows)],
+        after=(in_b,),
+        through=(in_a,),
+    )
+    in_a = in_a + got_in_a
+    sent_b, sent_a = held((sent_b, sent_a), (in_a,))
+    got_b, got_a = swap(sent_b, 1), swap(sent_a, 1)
+    in_a, got_in_a = z_halves(in_a)
+    ob, out_b, in_a, in_b = project(
+        up_grad, out_w, keep, got_b, out_tile, whole_b, after=(sent_a,), through=(in_a, in_b)
+    )
+    got_out_b = swap(ob, 2)
+    in_a = in_a + got_in_a
+    got_in_a = swap(in_a, 8)
+    in_b, got_z_b = z_halves(in_b + got_in_b)
+    oa, out_a, out_b, in_b = project(
+        up_grad, out_w, keep, got_a, out_tile, whole_a, after=(in_a,), through=(out_b, in_b)
+    )
+    in_b = in_b + got_z_b
+    (in_a,) = held((in_a + got_in_a,), (oa,))
+    (oa,) = held((oa,), (in_b,))
+    got_out_a = swap(oa, 2)
     in_a = z_whole(in_a)
-    out_b = z_halves(mb + swap(ob, 2))
     in_b = in_b + swap(in_b, 8)
-    out_a = ma + swap(oa, 2)
+    out_b, got_out_b = z_halves(out_b + got_out_b)
+    out_b = out_b + got_out_b
+    out_a = out_a + got_out_a
     example = jnp.stack([contract(in_a, out_a), contract(in_b, out_b)]).reshape(-1, LANES)
     for bit in (1, 4, 8):
         example = example + swap(example, bit)

time: 122 us -> 111 us (0.910)
  waiting for transfers between devices: 36 us -> 26.3 us
  Pallas kernels: 52.7 us -> 49.5 us
  other arithmetic: 4.8 us -> 6.32 us
    ppermute x17, waiting for transfers between devices: 36 us -> 26.3 us  [swap(): return lax.ppermute(value, 'store', [(i, i ^ bit) for i in range(16)])]
    pallas_call x6 -> x5, Pallas kernels: 51.1 us -> 47.9 us  [project(): pl.pallas_call(functools.partial(project_kernel, tile, cuts, add is not N...]
    add x6, other arithmetic: 3.48 us -> 5 us  [the longest x1 1.1 us: reduced_examples(): out_b, got_out_b = z_halves(out_b + got_out_b)]
    unnamed x26 -> x34, local copies, waits for them, and re-layouts: 5.56 us -> 5.69 us
  transfers between devices with their start and end apart: 17 -> 17, of which waited for: 10 -> 8; matrix products, arithmetic and copies ran while one was open for 6% -> 7% of each run, Pallas kernels for 28% -> 28%
where the time goes in v2:
time: 111 us; the launch traced here: 110 us
  Pallas kernels  49.5 us (45%)
  waiting for transfers between devices  26.3 us (24%)
  starting transfers between devices  16.5 us (15%)
  local copies, waits for them, and re-layouts  7.08 us (6%)
  other arithmetic  6.32 us (6%)
  matrix products  4.06 us (4%)
    pallas_call x5, Pallas kernels, project(): pl.pallas_call(functools.partial(project_kernel, tile, cuts, add is not N...  47.9 us
    ppermute x17, waiting for transfers between devices, swap(): return lax.ppermute(value, 'store', [(i, i ^ bit) for i in range(16)])  26.3 us
    ppermute x17, starting transfers between devices, swap(): return lax.ppermute(value, 'store', [(i, i ^ bit) for i in range(16)])  16.5 us
    unnamed x34, local copies, waits for them, and re-layouts  5.69 us
    dot_general x2, matrix products, contract(): lax.dot_general(left, right, (((0,), (0,)), ((), ())), precision=lax.Prec...  2.81 us
  transfers between devices with their start and end apart: 17, of which 8 were waited for; matrix products, arithmetic and copies ran while one was open for 7% of the time, Pallas kernels for 28%

profile of v2, /device:TPU:0, one launch (start us, length us, event | category | flops | bytes accessed | tf_op | source)
XLA Modules:
  0.0 109.9 jit_solution(10795235177179219658)
XLA Ops:
  0.1 11.0 %shard_map.73 = (f32[4096,128]{1,0:T(8,128)}, bf16[2,512,128]{2,1,0:T(8,128)(2,1)S(1)}) custom-call(s32[6]{0:T(128)S(1)} %stack.68.refs_0_, bf16[16384,512]{1,0:T(8,128)(2,1)} %refs_1_.6, s32[8,32]{1,0:T(8,128)} %refs_2_.1, bf16[256,8,32]{2,1,0:T(8,128)(2,1)} %bitcast.49), custom_call_target="tpu_custom_call" | custom-call | flops 268435456 | bytes 2097152 | tf_op jit(solution)/shard_map/pallas_call | solution.py:196
  12.3 1.6 %shard_map.74.refs_4_.refs_2_ = bf16[2,1792,128]{2,1,0:T(8,128)(2,1)S(1)} custom-call(s32[1]{0:T(128)} %bitcast.6.first_ref, s32[8,112]{1,0:T(8,128)S(1)} %copy-done.13, bf16[8,256,112]{2,1,0:T(8,128)(2,1)S(1)} %bitcast.42, f32[4096,128]{1,0:T(8,128)} %get-tuple-element.24.rest_0_), custom_call_target="tpu_custom_call" | custom-call | flops 1000000000 | bytes 458752 | tf_op jit(solution)/shard_map/pallas_call | solution.py:85
  13.9 2.4 %collective-permute-done.refs_3_ = f32[4096,128]{1,0:T(8,128)} collective-permute-done((f32[4096,128]{1,0:T(8,128)}, f32[4096,128]{1,0:T(8,128)}, u32[]{:S(2)}, u32[]{:S(2)}) %collective-permute-start) | collective-permute-done | bytes 2097184 | tf_op jit(solution)/shard_map/ppermute | solution.py:240
  16.3 7.8 %shard_map.75 = (f32[1024,128]{1,0:T(8,128)S(1)}, f32[1024,128]{1,0:T(8,128)S(1)}, f32[1024,128]{1,0:T(8,128)S(1)}, f32[1024,128]{1,0:T(8,128)S(1)}) custom-call(s32[6]{0:T(128)S(1)} %stack.66.refs_0_, bf16[16384,512]{1,0:T(8,128)(2,1)} %refs_1_.6, bf16[2,512,128]{2,1,0:T(8,128)(2,1)S(1)} %copy-done.10, f32[4096,128]{1,0:T(8,128)} %collective-permute-done.refs_3_, ...), custom_call_target="tpu_custom_call" | custom-call | flops 268435456 | bytes 2097152 | tf_op jit(solution)/shard_map/pallas_call | solution.py:196
  24.1 3.0 %collective-permute-start.1 = (f32[1024,128]{1,0:T(8,128)S(1)}, f32[1024,128]{1,0:T(8,128)S(1)}, u32[]{:S(2)}, u32[]{:S(2)}) collective-permute-start(f32[1024,128]{1,0:T(8,128)S(1)} %get-tuple-element.31), channel_id=1, source_target_pairs={{0,2},{1,3},{2,0},{3,1},{4,6},{5,7},{6,4},{7,5},{8,10},{9,11},{10,... | collective-permute-start | bytes 1572872 | tf_op jit(solution)/shard_map/ppermute | solution.py:240
  27.1 12.5 %shard_map.76 = (f32[2048,128]{1,0:T(8,128)S(1)}, f32[2048,128]{1,0:T(8,128)S(1)}, f32[1024,128]{1,0:T(8,128)S(1)}) custom-call(s32[6]{0:T(128)S(1)} %stack.68.refs_0_, bf16[16384,1792]{1,0:T(8,128)(2,1)} %refs_1_.9, bf16[2,1792,128]{2,1,0:T(8,128)(2,1)S(1)} %shard_map.74.refs_4_.refs_2_, ...), custom_call_target="tpu_custom_call", output_to_operand_aliasing={{2}: (4, {})} | custom-call | flops 939524096 | bytes 7340032 | tf_op jit(solution)/shard_map/pallas_call | solution.py:196
  43.5 2.0 %collective-permute-start.3 = (f32[512,128]{1,0:T(8,128)S(1)}, f32[512,128]{1,0:T(8,128)S(1)}, u32[]{:S(2)}, u32[]{:S(2)}) collective-permute-start(f32[512,128]{1,0:T(8,128)S(1)} %get-tuple-element.45), channel_id=1, source_target_pairs={{0,4},{1,5},{2,6},{3,7},{4,0},{5,1},{6,2},{7,3},{8,12},{9,13},{10,... | collective-permute-start | bytes 786440 | tf_op jit(solution)/shard_map/ppermute | solution.py:240
  45.5 1.2 %copy-done.2 = f32[2048,128]{1,0:T(8,128)S(1)} copy-done((f32[2048,128]{1,0:T(8,128)S(1)}, f32[2048,128]{1,0:T(8,128)}, u32[]{:S(2)}) %copy-start.2) | copy-done | bytes 1048600
  46.8 8.5 %shard_map.78 = (f32[1024,128]{1,0:T(8,128)}, f32[1024,128]{1,0:T(8,128)S(1)}, f32[512,128]{1,0:T(8,128)S(1)}, f32[1024,128]{1,0:T(8,128)S(1)}) custom-call(s32[6]{0:T(128)S(1)} %stack.66.refs_0_, bf16[16384,1792]{1,0:T(8,128)(2,1)} %refs_1_.9, bf16[2,1792,128]{2,1,0:T(8,128)(2,1)S(1)} %shard_map.74.refs_4_.refs_2_, ...), custom_call_target="tpu_custom_call", output_to_operand_aliasing={{2}: (5, {}), {3}: (6, {})} | custom-call | flops 469762048 | bytes 3670016 | tf_op jit(solution)/shard_map/pallas_call | solution.py:196
  55.2 1.7 %collective-permute-start.11 = (f32[1024,128]{1,0:T(8,128)}, f32[1024,128]{1,0:T(8,128)}, u32[]{:S(2)}, u32[]{:S(2)}) collective-permute-start(f32[1024,128]{1,0:T(8,128)} %get-tuple-element.42), channel_id=1, source_target_pairs={{0,2},{1,3},{2,0},{3,1},{4,6},{5,7},{6,4},{7,5},{8,10},{9,11},{10,... | collective-permute-start | bytes 1572872 | tf_op jit(solution)/shard_map/ppermute | solution.py:240
  56.9 2.6 %collective-permute-start.4 = (f32[512,128]{1,0:T(8,128)S(1)}, f32[512,128]{1,0:T(8,128)S(1)}, u32[]{:S(2)}, u32[]{:S(2)}) collective-permute-start(f32[512,128]{1,0:T(8,128)S(1)} %add.77.refs_4_), channel_id=1, source_target_pairs={{0,8},{1,9},{2,10},{3,11},{4,12},{5,13},{6,14},{7,15},{8,0},{9,1},... | collective-permute-start | bytes 786440 | tf_op jit(solution)/shard_map/ppermute | solution.py:240
  61.2 8.1 %shard_map.79 = (f32[1024,128]{1,0:T(8,128)S(1)}, f32[1024,128]{1,0:T(8,128)S(1)}, f32[1024,128]{1,0:T(8,128)S(1)}, f32[512,128]{1,0:T(8,128)S(1)}) custom-call(s32[6]{0:T(128)S(1)} %stack.66.refs_0_, bf16[16384,1792]{1,0:T(8,128)(2,1)} %refs_1_.9, ...), custom_call_target="tpu_custom_call", output_to_operand_aliasing={{2}: (5, {}), {3}: (6, {})} | custom-call | flops 469762048 | bytes 3670016 | tf_op jit(solution)/shard_map/pallas_call | solution.py:196
  71.8 1.6 %collective-permute-start.7 = (f32[512,128]{1,0:T(8,128)}, f32[512,128]{1,0:T(8,128)}, u32[]{:S(2)}, u32[]{:S(2)}) collective-permute-start(f32[512,128]{1,0:T(8,128)} %shard_map.80), channel_id=1, source_target_pairs={{0,4},{1,5},{2,6},{3,7},{4,0},{5,1},{6,2},{7,3},{8,12},{9,13},{10,... | collective-permute-start | bytes 786440 | tf_op jit(solution)/shard_map/ppermute | solution.py:240
  74.5 1.3 %collective-permute-start.10 = (f32[512,128]{1,0:T(8,128)S(1)}, f32[512,128]{1,0:T(8,128)}, u32[]{:S(2)}, u32[]{:S(2)}) collective-permute-start(f32[512,128]{1,0:T(8,128)S(1)} %add.80.refs_1_), channel_id=1, source_target_pairs={{0,8},{1,9},{2,10},{3,11},{4,12},{5,13},{6,14},{7,15},{8,0},{9,1},... | collective-permute-start | bytes 786440 | tf_op jit(solution)/shard_map/ppermute | solution.py:240
  77.8 1.6 %collective-permute-start.9 = (f32[1024,128]{1,0:T(8,128)}, f32[1024,128]{1,0:T(8,128)S(1)}, u32[]{:S(2)}, u32[]{:S(2)}) collective-permute-start(f32[1024,128]{1,0:T(8,128)} %shard_map.81), channel_id=1, source_target_pairs={{0,2},{1,3},{2,0},{3,1},{4,6},{5,7},{6,4},{7,5},{8,10},{9,11},{10,... | collective-permute-start | bytes 1572872 | tf_op jit(solution)/shard_map/ppermute | solution.py:240
  79.4 6.1 %collective-permute-done.7 = f32[512,128]{1,0:T(8,128)} collective-permute-done((f32[512,128]{1,0:T(8,128)}, f32[512,128]{1,0:T(8,128)}, u32[]{:S(2)}, u32[]{:S(2)}) %collective-permute-start.7) | collective-permute-done | bytes 262176 | tf_op jit(solution)/shard_map/ppermute | solution.py:240
  86.6 1.4 %collective-permute-done.10 = f32[512,128]{1,0:T(8,128)} collective-permute-done((f32[512,128]{1,0:T(8,128)S(1)}, f32[512,128]{1,0:T(8,128)}, u32[]{:S(2)}, u32[]{:S(2)}) %collective-permute-start.10) | collective-permute-done | bytes 262176 | tf_op jit(solution)/shard_map/ppermute | solution.py:240
  88.0 3.3 %collective-permute-done.12 = f32[512,128]{1,0:T(8,128)} collective-permute-done((f32[512,128]{1,0:T(8,128)S(1)}, f32[512,128]{1,0:T(8,128)}, u32[]{:S(2)}, u32[]{:S(2)}) %collective-permute-start.12) | collective-permute-done | bytes 262176 | tf_op jit(solution)/shard_map/ppermute | solution.py:240
  91.3 1.8 %fusion.2 = f32[128,128]{1,0:T(8,128)S(1)} fusion(f32[512,128]{1,0:T(8,128)} %collective-permute-done.12, f32[2,512,128]{2,1,0:T(8,128)} %bitcast.47, s32[]{:T(128)S(6)} %select_n.84, f32[512,128]{1,0:T(8,128)} %copy-done.14, f32[512,128]{1,0:T(8,128)} %collective-permute-done.10), kind=kOutput, calls=%fused_computation.4 | convolution fusion | flops 100794368 | bytes 1114116 | tf_op jit(solution)/shard_map/dot_general | solution.py:225
  94.4 1.2 %collective-permute-done.13 = f32[64,128]{1,0:T(8,128)S(1)} collective-permute-done((f32[64,128]{1,0:T(8,128)S(1)}, f32[64,128]{1,0:T(8,128)S(1)}, u32[]{:S(2)}, u32[]{:S(2)}) %collective-permute-start.13) | collective-permute-done | bytes 32800 | tf_op jit(solution)/shard_map/ppermute | solution.py:240
  96.1 3.4 %collective-permute-done.14 = f32[64,128]{1,0:T(8,128)S(1)} collective-permute-done((f32[64,128]{1,0:T(8,128)S(1)}, f32[64,128]{1,0:T(8,128)S(1)}, u32[]{:S(2)}, u32[]{:S(2)}) %collective-permute-start.14) | collective-permute-done | bytes 32800 | tf_op jit(solution)/shard_map/ppermute | solution.py:240
  100.0 4.7 %collective-permute-done.15 = f32[64,128]{1,0:T(8,128)S(1)} collective-permute-done((f32[64,128]{1,0:T(8,128)S(1)}, f32[64,128]{1,0:T(8,128)S(1)}, u32[]{:S(2)}, u32[]{:S(2)}) %collective-permute-start.15) | collective-permute-done | bytes 32800 | tf_op jit(solution)/shard_map/ppermute | solution.py:240
  104.9 3.7 %collective-permute-done.16 = f32[64,128]{1,0:T(8,128)S(1)} collective-permute-done((f32[64,128]{1,0:T(8,128)S(1)}, f32[64,128]{1,0:T(8,128)S(1)}, u32[]{:S(2)}, u32[]{:S(2)}) %collective-permute-start.16) | collective-permute-done | bytes 32800 | tf_op jit(solution)/shard_map/ppermute | solution.py:240
  108.7 1.2 %fusion.9 = f32[4,256]{1,0:T(4,128)} fusion(bf16[4,4096]{1,0:T(4,128)(2,1)S(1)} %convert_element_type.7, bf16[256,4096]{1,0:T(8,128)(2,1)S(1)} %copy-done), kind=kOutput, calls=%fused_computation.22 | convolution fusion | flops 8388608 | bytes 2134016 | tf_op jit(solution)/shard_map/dot_general | solution.py:356
  (78 shorter events, 16.0 us)
Async XLA Ops:
  0.0 108.7 %copy-start = (bf16[256,4096]{1,0:T(8,128)(2,1)S(1)}, bf16[256,4096]{1,0:T(8,128)(2,1)}, u32[]{:S(2)}) copy-start(bf16[256,4096]{1,0:T(8,128)(2,1)} %param.13) | copy-start | bytes 6291460
  0.1 12.2 %copy-start.11 = (bf16[8,112,32,8]{1,3,2,0:T(8,128)(2,1)S(1)}, bf16[8,112,32,8]{1,3,2,0:T(8,128)(2,1)}, u32[]{:S(2)}) copy-start(bf16[8,112,32,8]{1,3,2,0:T(8,128)(2,1)} %param.12) | copy-start | bytes 1376260
  0.1 12.2 %copy-start.13 = (s32[8,112]{1,0:T(8,128)S(1)}, s32[8,112]{1,0:T(8,128)}, u32[]{:S(2)}) copy-start(s32[8,112]{1,0:T(8,128)} %index_ref.1) | copy-start | bytes 10756
  11.8 4.5 %collective-permute-start = (f32[4096,128]{1,0:T(8,128)}, f32[4096,128]{1,0:T(8,128)}, u32[]{:S(2)}, u32[]{:S(2)}) collective-permute-start(f32[4096,128]{1,0:T(8,128)} %get-tuple-element.24.rest_0_), channel_id=1, source_target_pairs={{0,1},{1,0},{2,3},{3,2},{4,5},{5,4},{6,7},{7,6},{8,9},{9,8},{10,11... | collective-permute-start | bytes 6291464 | tf_op jit(solution)/shard_map/ppermute | solution.py:240
  12.3 4.0 %copy-start.10 = (bf16[2,512,128]{2,1,0:T(8,128)(2,1)S(1)}, bf16[2,512,128]{2,1,0:T(8,128)(2,1)}, u32[]{:S(2)}) copy-start(bf16[2,512,128]{2,1,0:T(8,128)(2,1)} %copy-done.9) | copy-start | bytes 786436
  24.1 15.5 %copy-start.12 = (f32[1024,128]{1,0:T(8,128)}, f32[1024,128]{1,0:T(8,128)S(1)}, u32[]{:S(2)}) copy-start(f32[1024,128]{1,0:T(8,128)S(1)} %get-tuple-element.37) | copy-start | bytes 1572868
  24.1 16.5 %collective-permute-start.1 = (f32[1024,128]{1,0:T(8,128)S(1)}, f32[1024,128]{1,0:T(8,128)S(1)}, u32[]{:S(2)}, u32[]{:S(2)}) collective-permute-start(f32[1024,128]{1,0:T(8,128)S(1)} %get-tuple-element.31), channel_id=1, source_target_pairs={{0,2},{1,3},{2,0},{3,1},{4,6},{5,7},{6,4},{7,5},{8,10},{9,11},{10,... | collective-permute-start | bytes 1572872 | tf_op jit(solution)/shard_map/ppermute | solution.py:240
  41.9 3.7 %collective-permute-start.2 = (f32[2048,128]{1,0:T(8,128)}, f32[2048,128]{1,0:T(8,128)}, u32[]{:S(2)}, u32[]{:S(2)}) collective-permute-start(f32[2048,128]{1,0:T(8,128)} %get-tuple-element.32), channel_id=1, source_target_pairs={{0,1},{1,0},{2,3},{3,2},{4,5},{5,4},{6,7},{7,6},{8,9},{9,8},{10,11... | collective-permute-start | bytes 3145736 | tf_op jit(solution)/shard_map/ppermute | solution.py:240
  41.9 19.3 %collective-permute-start.5 = (f32[2048,128]{1,0:T(8,128)}, f32[2048,128]{1,0:T(8,128)}, u32[]{:S(2)}, u32[]{:S(2)}) collective-permute-start(f32[2048,128]{1,0:T(8,128)} %get-tuple-element.33.refs_4_), channel_id=1, source_target_pairs={{0,1},{1,0},{2,3},{3,2},{4,5},{5,4},{6,7},{7,6},{8,9},{9,8},{10,11... | collective-permute-start | bytes 3145736 | tf_op jit(solution)/shard_map/ppermute | solution.py:240
  42.4 17.2 %collective-permute-start.6 = (f32[1024,128]{1,0:T(8,128)}, f32[1024,128]{1,0:T(8,128)}, u32[]{:S(2)}, u32[]{:S(2)}) collective-permute-start(f32[1024,128]{1,0:T(8,128)} %copy-done.12), channel_id=1, source_target_pairs={{0,2},{1,3},{2,0},{3,1},{4,6},{5,7},{6,4},{7,5},{8,10},{9,11},{10,... | collective-permute-start | bytes 1572872 | tf_op jit(solution)/shard_map/ppermute | solution.py:240
  43.5 13.3 %collective-permute-start.3 = (f32[512,128]{1,0:T(8,128)S(1)}, f32[512,128]{1,0:T(8,128)S(1)}, u32[]{:S(2)}, u32[]{:S(2)}) collective-permute-start(f32[512,128]{1,0:T(8,128)S(1)} %get-tuple-element.45), channel_id=1, source_target_pairs={{0,4},{1,5},{2,6},{3,7},{4,0},{5,1},{6,2},{7,3},{8,12},{9,13},{10,... | collective-permute-start | bytes 786440 | tf_op jit(solution)/shard_map/ppermute | solution.py:240
  55.2 20.6 %collective-permute-start.11 = (f32[1024,128]{1,0:T(8,128)}, f32[1024,128]{1,0:T(8,128)}, u32[]{:S(2)}, u32[]{:S(2)}) collective-permute-start(f32[1024,128]{1,0:T(8,128)} %get-tuple-element.42), channel_id=1, source_target_pairs={{0,2},{1,3},{2,0},{3,1},{4,6},{5,7},{6,4},{7,5},{8,10},{9,11},{10,... | collective-permute-start | bytes 1572872 | tf_op jit(solution)/shard_map/ppermute | solution.py:240
  56.9 14.0 %collective-permute-start.4 = (f32[512,128]{1,0:T(8,128)S(1)}, f32[512,128]{1,0:T(8,128)S(1)}, u32[]{:S(2)}, u32[]{:S(2)}) collective-permute-start(f32[512,128]{1,0:T(8,128)S(1)} %add.77.refs_4_), channel_id=1, source_target_pairs={{0,8},{1,9},{2,10},{3,11},{4,12},{5,13},{6,14},{7,15},{8,0},{9,1},... | collective-permute-start | bytes 786440 | tf_op jit(solution)/shard_map/ppermute | solution.py:240
  60.7 12.8 %collective-permute-start.8 = (f32[512,128]{1,0:T(8,128)S(1)}, f32[512,128]{1,0:T(8,128)}, u32[]{:S(2)}, u32[]{:S(2)}) collective-permute-start(f32[512,128]{1,0:T(8,128)S(1)} %get-tuple-element.43), channel_id=1, source_target_pairs={{0,4},{1,5},{2,6},{3,7},{4,0},{5,1},{6,2},{7,3},{8,12},{9,13},{10,... | collective-permute-start | bytes 786440 | tf_op jit(solution)/shard_map/ppermute | solution.py:240
  71.8 13.7 %collective-permute-start.7 = (f32[512,128]{1,0:T(8,128)}, f32[512,128]{1,0:T(8,128)}, u32[]{:S(2)}, u32[]{:S(2)}) collective-permute-start(f32[512,128]{1,0:T(8,128)} %shard_map.80), channel_id=1, source_target_pairs={{0,4},{1,5},{2,6},{3,7},{4,0},{5,1},{6,2},{7,3},{8,12},{9,13},{10,... | collective-permute-start | bytes 786440 | tf_op jit(solution)/shard_map/ppermute | solution.py:240
  73.5 12.0 %copy-start.15 = (f32[512,128]{1,0:T(8,128)S(1)}, f32[512,128]{1,0:T(8,128)}, u32[]{:S(2)}) copy-start(f32[512,128]{1,0:T(8,128)} %shard_map.80) | copy-start | bytes 786436
  74.5 13.4 %collective-permute-start.10 = (f32[512,128]{1,0:T(8,128)S(1)}, f32[512,128]{1,0:T(8,128)}, u32[]{:S(2)}, u32[]{:S(2)}) collective-permute-start(f32[512,128]{1,0:T(8,128)S(1)} %add.80.refs_1_), channel_id=1, source_target_pairs={{0,8},{1,9},{2,10},{3,11},{4,12},{5,13},{6,14},{7,15},{8,0},{9,1},... | collective-permute-start | bytes 786440 | tf_op jit(solution)/shard_map/ppermute | solution.py:240
  76.9 16.3 %copy-start.8 = (f32[1024,128]{1,0:T(8,128)S(1)}, f32[1024,128]{1,0:T(8,128)}, u32[]{:S(2)}) copy-start(f32[1024,128]{1,0:T(8,128)} %copy-done.7) | copy-start | bytes 1572868
  77.7 13.6 %collective-permute-start.12 = (f32[512,128]{1,0:T(8,128)S(1)}, f32[512,128]{1,0:T(8,128)}, u32[]{:S(2)}, u32[]{:S(2)}) collective-permute-start(f32[512,128]{1,0:T(8,128)S(1)} %dynamic-slice_bitcast_fusion), channel_id=1, source_target_pairs={{0,4},{1,5},{2,6},{3,7},{4,0},{5,1},{6,2},{7,3},{8,12},{9,13},{10,... | collective-permute-start | bytes 786440 | tf_op jit(solution)/shard_map/ppermute | solution.py:240
  77.8 15.3 %collective-permute-start.9 = (f32[1024,128]{1,0:T(8,128)}, f32[1024,128]{1,0:T(8,128)S(1)}, u32[]{:S(2)}, u32[]{:S(2)}) collective-permute-start(f32[1024,128]{1,0:T(8,128)} %shard_map.81), channel_id=1, source_target_pairs={{0,2},{1,3},{2,0},{3,1},{4,6},{5,7},{6,4},{7,5},{8,10},{9,11},{10,... | collective-permute-start | bytes 1572872 | tf_op jit(solution)/shard_map/ppermute | solution.py:240
  94.4 1.2 %collective-permute-start.13 = (f32[64,128]{1,0:T(8,128)S(1)}, f32[64,128]{1,0:T(8,128)S(1)}, u32[]{:S(2)}, u32[]{:S(2)}) collective-permute-start(f32[64,128]{1,0:T(8,128)S(1)} %reshape.72), channel_id=1, source_target_pairs={{0,1},{1,0},{2,3},{3,2},{4,5},{5,4},{6,7},{7,6},{8,9},{9,8},{10,11... | collective-permute-start | bytes 98312 | tf_op jit(solution)/shard_map/ppermute | solution.py:240
  95.6 3.9 %collective-permute-start.14 = (f32[64,128]{1,0:T(8,128)S(1)}, f32[64,128]{1,0:T(8,128)S(1)}, u32[]{:S(2)}, u32[]{:S(2)}) collective-permute-start(f32[64,128]{1,0:T(8,128)S(1)} %add.87), channel_id=1, source_target_pairs={{0,4},{1,5},{2,6},{3,7},{4,0},{5,1},{6,2},{7,3},{8,12},{9,13},{10,... | collective-permute-start | bytes 98312 | tf_op jit(solution)/shard_map/ppermute | solution.py:240
  99.5 5.1 %collective-permute-start.15 = (f32[64,128]{1,0:T(8,128)S(1)}, f32[64,128]{1,0:T(8,128)S(1)}, u32[]{:S(2)}, u32[]{:S(2)}) collective-permute-start(f32[64,128]{1,0:T(8,128)S(1)} %add.88), channel_id=1, source_target_pairs={{0,8},{1,9},{2,10},{3,11},{4,12},{5,13},{6,14},{7,15},{8,0},{9,1},... | collective-permute-start | bytes 98312 | tf_op jit(solution)/shard_map/ppermute | solution.py:240
  104.6 3.9 %collective-permute-start.16 = (f32[64,128]{1,0:T(8,128)S(1)}, f32[64,128]{1,0:T(8,128)S(1)}, u32[]{:S(2)}, u32[]{:S(2)}) collective-permute-start(f32[64,128]{1,0:T(8,128)S(1)} %add.89), channel_id=1, source_target_pairs={{0,2},{1,3},{2,0},{3,1},{4,6},{5,7},{6,4},{7,5},{8,10},{9,11},{10,... | collective-permute-start | bytes 98312 | tf_op jit(solution)/shard_map/ppermute | solution.py:240
  (10 other events, 14.8 us)

commit v3 on v2

--- a/solution.py
+++ b/solution.py
@@ -311,8 +311,8 @@
     out_b = out_b + got_out_b
     out_a = out_a + got_out_a
     example = jnp.stack([contract(in_a, out_a), contract(in_b, out_b)]).reshape(-1, LANES)
-    for bit in (1, 4, 8):
-        example = example + swap(example, bit)
+    example = example + swap(example, 1)
+    example = example + swap(example, 4) + swap(example, 8) + swap(example, 12)
     other = swap(example, 2)
     example, other = example.reshape(2, HALF * HALF), other.reshape(2, HALF * HALF)
     first = jnp.where(x == 0, example, other)

time: 111 us -> 108 us (0.973)
  waiting for transfers between devices: 26.3 us -> 18.8 us
  starting transfers between devices: 16.5 us -> 21.9 us
    ppermute x17 -> x18, waiting for transfers between devices: 26.3 us -> 18.8 us  [swap(): return lax.ppermute(value, 'store', [(i, i ^ bit) for i in range(16)])]
    ppermute x17 -> x18, starting transfers between devices: 16.5 us -> 21.9 us  [swap(): return lax.ppermute(value, 'store', [(i, i ^ bit) for i in range(16)])]
  transfers between devices with their start and end apart: 17 -> 18, of which waited for: 8 -> 9; matrix products, arithmetic and copies ran while one was open for 7% -> 8% of each run, Pallas kernels for 28% -> 28%
where the time goes in v3:
time: 108 us
  Pallas kernels  49.4 us (46%)
  starting transfers between devices  21.9 us (20%)
  waiting for transfers between devices  18.8 us (17%)
  local copies, waits for them, and re-layouts  7.04 us (7%)
  other arithmetic  6.31 us (6%)
  matrix products  4.06 us (4%)
    pallas_call x5, Pallas kernels, project(): pl.pallas_call(functools.partial(project_kernel, tile, cuts, add is not N...  47.8 us
    ppermute x18, starting transfers between devices, swap(): return lax.ppermute(value, 'store', [(i, i ^ bit) for i in range(16)])  21.9 us
    ppermute x18, waiting for transfers between devices, swap(): return lax.ppermute(value, 'store', [(i, i ^ bit) for i in range(16)])  18.8 us
    unnamed x34, local copies, waits for them, and re-layouts  5.66 us
    dot_general x2, matrix products, contract(): lax.dot_general(left, right, (((0,), (0,)), ((), ())), precision=lax.Prec...  2.81 us
  transfers between devices with their start and end apart: 18, of which 9 were waited for; matrix products, arithmetic and copies ran while one was open for 8% of the time, Pallas kernels for 28%

profile of v3, /device:TPU:0, one launch (start us, length us, event | category | flops | bytes accessed | tf_op | source)
XLA Modules:
  0.0 107.8 jit_solution(9797635810819142061)
XLA Ops:
  0.1 11.0 %shard_map.73 = (f32[4096,128]{1,0:T(8,128)}, bf16[2,512,128]{2,1,0:T(8,128)(2,1)S(1)}) custom-call(s32[6]{0:T(128)S(1)} %stack.68.refs_0_, bf16[16384,512]{1,0:T(8,128)(2,1)} %refs_1_.6, s32[8,32]{1,0:T(8,128)} %refs_2_.1, bf16[256,8,32]{2,1,0:T(8,128)(2,1)} %bitcast.49), custom_call_target="tpu_custom_call" | custom-call | flops 268435456 | bytes 2097152 | tf_op jit(solution)/shard_map/pallas_call | solution.py:196
  12.3 1.6 %shard_map.74.refs_4_.refs_2_ = bf16[2,1792,128]{2,1,0:T(8,128)(2,1)S(1)} custom-call(s32[1]{0:T(128)} %bitcast.6.first_ref, s32[8,112]{1,0:T(8,128)S(1)} %copy-done.13, bf16[8,256,112]{2,1,0:T(8,128)(2,1)S(1)} %bitcast.42, f32[4096,128]{1,0:T(8,128)} %get-tuple-element.24.rest_0_), custom_call_target="tpu_custom_call" | custom-call | flops 1000000000 | bytes 458752 | tf_op jit(solution)/shard_map/pallas_call | solution.py:85
  13.9 2.4 %collective-permute-done.refs_3_ = f32[4096,128]{1,0:T(8,128)} collective-permute-done((f32[4096,128]{1,0:T(8,128)}, f32[4096,128]{1,0:T(8,128)}, u32[]{:S(2)}, u32[]{:S(2)}) %collective-permute-start) | collective-permute-done | bytes 2097184 | tf_op jit(solution)/shard_map/ppermute | solution.py:240
  16.3 7.8 %shard_map.75 = (f32[1024,128]{1,0:T(8,128)S(1)}, f32[1024,128]{1,0:T(8,128)S(1)}, f32[1024,128]{1,0:T(8,128)S(1)}, f32[1024,128]{1,0:T(8,128)S(1)}) custom-call(s32[6]{0:T(128)S(1)} %stack.66.refs_0_, bf16[16384,512]{1,0:T(8,128)(2,1)} %refs_1_.6, bf16[2,512,128]{2,1,0:T(8,128)(2,1)S(1)} %copy-done.10, f32[4096,128]{1,0:T(8,128)} %collective-permute-done.refs_3_, ...), custom_call_target="tpu_custom_call" | custom-call | flops 268435456 | bytes 2097152 | tf_op jit(solution)/shard_map/pallas_call | solution.py:196
  24.1 2.9 %collective-permute-start.1 = (f32[1024,128]{1,0:T(8,128)S(1)}, f32[1024,128]{1,0:T(8,128)S(1)}, u32[]{:S(2)}, u32[]{:S(2)}) collective-permute-start(f32[1024,128]{1,0:T(8,128)S(1)} %get-tuple-element.31), channel_id=1, source_target_pairs={{0,2},{1,3},{2,0},{3,1},{4,6},{5,7},{6,4},{7,5},{8,10},{9,11},{10,... | collective-permute-start | bytes 1572872 | tf_op jit(solution)/shard_map/ppermute | solution.py:240
  27.0 12.5 %shard_map.76 = (f32[2048,128]{1,0:T(8,128)S(1)}, f32[2048,128]{1,0:T(8,128)S(1)}, f32[1024,128]{1,0:T(8,128)S(1)}) custom-call(s32[6]{0:T(128)S(1)} %stack.68.refs_0_, bf16[16384,1792]{1,0:T(8,128)(2,1)} %refs_1_.9, bf16[2,1792,128]{2,1,0:T(8,128)(2,1)S(1)} %shard_map.74.refs_4_.refs_2_, ...), custom_call_target="tpu_custom_call", output_to_operand_aliasing={{2}: (4, {})} | custom-call | flops 939524096 | bytes 7340032 | tf_op jit(solution)/shard_map/pallas_call | solution.py:196
  43.4 2.2 %collective-permute-start.3 = (f32[512,128]{1,0:T(8,128)S(1)}, f32[512,128]{1,0:T(8,128)S(1)}, u32[]{:S(2)}, u32[]{:S(2)}) collective-permute-start(f32[512,128]{1,0:T(8,128)S(1)} %get-tuple-element.45), channel_id=1, source_target_pairs={{0,4},{1,5},{2,6},{3,7},{4,0},{5,1},{6,2},{7,3},{8,12},{9,13},{10,... | collective-permute-start | bytes 786440 | tf_op jit(solution)/shard_map/ppermute | solution.py:240
  45.6 1.2 %copy-done.2 = f32[2048,128]{1,0:T(8,128)S(1)} copy-done((f32[2048,128]{1,0:T(8,128)S(1)}, f32[2048,128]{1,0:T(8,128)}, u32[]{:S(2)}) %copy-start.2) | copy-done | bytes 1048600
  46.9 8.5 %shard_map.78 = (f32[1024,128]{1,0:T(8,128)}, f32[1024,128]{1,0:T(8,128)S(1)}, f32[512,128]{1,0:T(8,128)S(1)}, f32[1024,128]{1,0:T(8,128)S(1)}) custom-call(s32[6]{0:T(128)S(1)} %stack.66.refs_0_, bf16[16384,1792]{1,0:T(8,128)(2,1)} %refs_1_.9, bf16[2,1792,128]{2,1,0:T(8,128)(2,1)S(1)} %shard_map.74.refs_4_.refs_2_, ...), custom_call_target="tpu_custom_call", output_to_operand_aliasing={{2}: (5, {}), {3}: (6, {})} | custom-call | flops 469762048 | bytes 3670016 | tf_op jit(solution)/shard_map/pallas_call | solution.py:196
  55.3 1.5 %collective-permute-start.11 = (f32[1024,128]{1,0:T(8,128)}, f32[1024,128]{1,0:T(8,128)}, u32[]{:S(2)}, u32[]{:S(2)}) collective-permute-start(f32[1024,128]{1,0:T(8,128)} %get-tuple-element.42), channel_id=1, source_target_pairs={{0,2},{1,3},{2,0},{3,1},{4,6},{5,7},{6,4},{7,5},{8,10},{9,11},{10,... | collective-permute-start | bytes 1572872 | tf_op jit(solution)/shard_map/ppermute | solution.py:240
  56.9 2.6 %collective-permute-start.4 = (f32[512,128]{1,0:T(8,128)S(1)}, f32[512,128]{1,0:T(8,128)S(1)}, u32[]{:S(2)}, u32[]{:S(2)}) collective-permute-start(f32[512,128]{1,0:T(8,128)S(1)} %add.80.refs_4_), channel_id=1, source_target_pairs={{0,8},{1,9},{2,10},{3,11},{4,12},{5,13},{6,14},{7,15},{8,0},{9,1},... | collective-permute-start | bytes 786440 | tf_op jit(solution)/shard_map/ppermute | solution.py:240
  61.2 8.1 %shard_map.79 = (f32[1024,128]{1,0:T(8,128)S(1)}, f32[1024,128]{1,0:T(8,128)S(1)}, f32[1024,128]{1,0:T(8,128)S(1)}, f32[512,128]{1,0:T(8,128)S(1)}) custom-call(s32[6]{0:T(128)S(1)} %stack.66.refs_0_, bf16[16384,1792]{1,0:T(8,128)(2,1)} %refs_1_.9, ...), custom_call_target="tpu_custom_call", output_to_operand_aliasing={{2}: (5, {}), {3}: (6, {})} | custom-call | flops 469762048 | bytes 3670016 | tf_op jit(solution)/shard_map/pallas_call | solution.py:196
  71.8 1.5 %collective-permute-start.7 = (f32[512,128]{1,0:T(8,128)}, f32[512,128]{1,0:T(8,128)}, u32[]{:S(2)}, u32[]{:S(2)}) collective-permute-start(f32[512,128]{1,0:T(8,128)} %shard_map.80), channel_id=1, source_target_pairs={{0,4},{1,5},{2,6},{3,7},{4,0},{5,1},{6,2},{7,3},{8,12},{9,13},{10,... | collective-permute-start | bytes 786440 | tf_op jit(solution)/shard_map/ppermute | solution.py:240
  74.4 1.5 %collective-permute-start.10 = (f32[512,128]{1,0:T(8,128)S(1)}, f32[512,128]{1,0:T(8,128)}, u32[]{:S(2)}, u32[]{:S(2)}) collective-permute-start(f32[512,128]{1,0:T(8,128)S(1)} %add.83.refs_1_), channel_id=1, source_target_pairs={{0,8},{1,9},{2,10},{3,11},{4,12},{5,13},{6,14},{7,15},{8,0},{9,1},... | collective-permute-start | bytes 786440 | tf_op jit(solution)/shard_map/ppermute | solution.py:240
  77.9 1.6 %collective-permute-start.9 = (f32[1024,128]{1,0:T(8,128)}, f32[1024,128]{1,0:T(8,128)S(1)}, u32[]{:S(2)}, u32[]{:S(2)}) collective-permute-start(f32[1024,128]{1,0:T(8,128)} %shard_map.81), channel_id=1, source_target_pairs={{0,2},{1,3},{2,0},{3,1},{4,6},{5,7},{6,4},{7,5},{8,10},{9,11},{10,... | collective-permute-start | bytes 1572872 | tf_op jit(solution)/shard_map/ppermute | solution.py:240
  79.4 6.6 %collective-permute-done.7 = f32[512,128]{1,0:T(8,128)} collective-permute-done((f32[512,128]{1,0:T(8,128)}, f32[512,128]{1,0:T(8,128)}, u32[]{:S(2)}, u32[]{:S(2)}) %collective-permute-start.7) | collective-permute-done | bytes 262176 | tf_op jit(solution)/shard_map/ppermute | solution.py:240
  87.7 3.5 %collective-permute-done.12 = f32[512,128]{1,0:T(8,128)} collective-permute-done((f32[512,128]{1,0:T(8,128)S(1)}, f32[512,128]{1,0:T(8,128)}, u32[]{:S(2)}, u32[]{:S(2)}) %collective-permute-start.12) | collective-permute-done | bytes 262176 | tf_op jit(solution)/shard_map/ppermute | solution.py:240
  91.3 1.8 %fusion.2 = f32[128,128]{1,0:T(8,128)S(1)} fusion(f32[512,128]{1,0:T(8,128)} %collective-permute-done.12, f32[2,512,128]{2,1,0:T(8,128)} %bitcast.47, s32[]{:T(128)S(6)} %select_n.84, f32[512,128]{1,0:T(8,128)} %copy-done.14, f32[512,128]{1,0:T(8,128)} %collective-permute-done.10), kind=kOutput, calls=%fused_computation.4 | convolution fusion | flops 100794368 | bytes 1114116 | tf_op jit(solution)/shard_map/dot_general | solution.py:225
  95.6 1.8 %collective-permute-start.16 = (f32[64,128]{1,0:T(8,128)S(1)}, f32[64,128]{1,0:T(8,128)S(1)}, u32[]{:S(2)}, u32[]{:S(2)}) collective-permute-start(f32[64,128]{1,0:T(8,128)S(1)} %add.90), channel_id=1, source_target_pairs={{0,12},{1,13},{2,14},{3,15},{4,8},{5,9},{6,10},{7,11},{8,4},{9,5},... | collective-permute-start | bytes 98312 | tf_op jit(solution)/shard_map/ppermute | solution.py:240
  97.4 2.5 %collective-permute-start.14 = (f32[64,128]{1,0:T(8,128)S(1)}, f32[64,128]{1,0:T(8,128)S(1)}, u32[]{:S(2)}, u32[]{:S(2)}) collective-permute-start(f32[64,128]{1,0:T(8,128)S(1)} %add.90), channel_id=1, source_target_pairs={{0,4},{1,5},{2,6},{3,7},{4,0},{5,1},{6,2},{7,3},{8,12},{9,13},{10,... | collective-permute-start | bytes 98312 | tf_op jit(solution)/shard_map/ppermute | solution.py:240
  100.0 1.3 %collective-permute-done.16 = f32[64,128]{1,0:T(8,128)S(1)} collective-permute-done((f32[64,128]{1,0:T(8,128)S(1)}, f32[64,128]{1,0:T(8,128)S(1)}, u32[]{:S(2)}, u32[]{:S(2)}) %collective-permute-start.16) | collective-permute-done | bytes 32800 | tf_op jit(solution)/shard_map/ppermute | solution.py:240
  102.5 2.1 %collective-permute-start.17 = (f32[64,128]{1,0:T(8,128)S(1)}, f32[64,128]{1,0:T(8,128)S(1)}, u32[]{:S(2)}, u32[]{:S(2)}) collective-permute-start(f32[64,128]{1,0:T(8,128)S(1)} %add_add_fusion), channel_id=1, source_target_pairs={{0,2},{1,3},{2,0},{3,1},{4,6},{5,7},{6,4},{7,5},{8,10},{9,11},{10,... | collective-permute-start | bytes 98312 | tf_op jit(solution)/shard_map/ppermute | solution.py:240
  104.5 1.9 %collective-permute-done.17 = f32[64,128]{1,0:T(8,128)S(1)} collective-permute-done((f32[64,128]{1,0:T(8,128)S(1)}, f32[64,128]{1,0:T(8,128)S(1)}, u32[]{:S(2)}, u32[]{:S(2)}) %collective-permute-start.17) | collective-permute-done | bytes 32800 | tf_op jit(solution)/shard_map/ppermute | solution.py:240
  106.6 1.2 %fusion.9 = f32[4,256]{1,0:T(4,128)} fusion(bf16[4,4096]{1,0:T(4,128)(2,1)S(1)} %convert_element_type.7, bf16[256,4096]{1,0:T(8,128)(2,1)S(1)} %copy-done), kind=kOutput, calls=%fused_computation.23 | convolution fusion | flops 8388608 | bytes 2134016 | tf_op jit(solution)/shard_map/dot_general | solution.py:356
  (79 shorter events, 18.0 us)
Async XLA Ops:
  0.0 106.6 %copy-start = (bf16[256,4096]{1,0:T(8,128)(2,1)S(1)}, bf16[256,4096]{1,0:T(8,128)(2,1)}, u32[]{:S(2)}) copy-start(bf16[256,4096]{1,0:T(8,128)(2,1)} %param.13) | copy-start | bytes 6291460
  0.1 12.2 %copy-start.11 = (bf16[8,112,32,8]{1,3,2,0:T(8,128)(2,1)S(1)}, bf16[8,112,32,8]{1,3,2,0:T(8,128)(2,1)}, u32[]{:S(2)}) copy-start(bf16[8,112,32,8]{1,3,2,0:T(8,128)(2,1)} %param.12) | copy-start | bytes 1376260
  0.1 12.2 %copy-start.13 = (s32[8,112]{1,0:T(8,128)S(1)}, s32[8,112]{1,0:T(8,128)}, u32[]{:S(2)}) copy-start(s32[8,112]{1,0:T(8,128)} %index_ref.1) | copy-start | bytes 10756
  11.8 4.5 %collective-permute-start = (f32[4096,128]{1,0:T(8,128)}, f32[4096,128]{1,0:T(8,128)}, u32[]{:S(2)}, u32[]{:S(2)}) collective-permute-start(f32[4096,128]{1,0:T(8,128)} %get-tuple-element.24.rest_0_), channel_id=1, source_target_pairs={{0,1},{1,0},{2,3},{3,2},{4,5},{5,4},{6,7},{7,6},{8,9},{9,8},{10,11... | collective-permute-start | bytes 6291464 | tf_op jit(solution)/shard_map/ppermute | solution.py:240
  24.1 15.5 %copy-start.12 = (f32[1024,128]{1,0:T(8,128)}, f32[1024,128]{1,0:T(8,128)S(1)}, u32[]{:S(2)}) copy-start(f32[1024,128]{1,0:T(8,128)S(1)} %get-tuple-element.37) | copy-start | bytes 1572868
  24.1 16.5 %collective-permute-start.1 = (f32[1024,128]{1,0:T(8,128)S(1)}, f32[1024,128]{1,0:T(8,128)S(1)}, u32[]{:S(2)}, u32[]{:S(2)}) collective-permute-start(f32[1024,128]{1,0:T(8,128)S(1)} %get-tuple-element.31), channel_id=1, source_target_pairs={{0,2},{1,3},{2,0},{3,1},{4,6},{5,7},{6,4},{7,5},{8,10},{9,11},{10,... | collective-permute-start | bytes 1572872 | tf_op jit(solution)/shard_map/ppermute | solution.py:240
  41.8 3.9 %collective-permute-start.2 = (f32[2048,128]{1,0:T(8,128)}, f32[2048,128]{1,0:T(8,128)}, u32[]{:S(2)}, u32[]{:S(2)}) collective-permute-start(f32[2048,128]{1,0:T(8,128)} %get-tuple-element.32), channel_id=1, source_target_pairs={{0,1},{1,0},{2,3},{3,2},{4,5},{5,4},{6,7},{7,6},{8,9},{9,8},{10,11... | collective-permute-start | bytes 3145736 | tf_op jit(solution)/shard_map/ppermute | solution.py:240
  41.8 19.4 %collective-permute-start.5 = (f32[2048,128]{1,0:T(8,128)}, f32[2048,128]{1,0:T(8,128)}, u32[]{:S(2)}, u32[]{:S(2)}) collective-permute-start(f32[2048,128]{1,0:T(8,128)} %get-tuple-element.33.refs_4_), channel_id=1, source_target_pairs={{0,1},{1,0},{2,3},{3,2},{4,5},{5,4},{6,7},{7,6},{8,9},{9,8},{10,11... | collective-permute-start | bytes 3145736 | tf_op jit(solution)/shard_map/ppermute | solution.py:240
  42.3 17.2 %collective-permute-start.6 = (f32[1024,128]{1,0:T(8,128)}, f32[1024,128]{1,0:T(8,128)}, u32[]{:S(2)}, u32[]{:S(2)}) collective-permute-start(f32[1024,128]{1,0:T(8,128)} %copy-done.12), channel_id=1, source_target_pairs={{0,2},{1,3},{2,0},{3,1},{4,6},{5,7},{6,4},{7,5},{8,10},{9,11},{10,... | collective-permute-start | bytes 1572872 | tf_op jit(solution)/shard_map/ppermute | solution.py:240
  43.4 13.4 %collective-permute-start.3 = (f32[512,128]{1,0:T(8,128)S(1)}, f32[512,128]{1,0:T(8,128)S(1)}, u32[]{:S(2)}, u32[]{:S(2)}) collective-permute-start(f32[512,128]{1,0:T(8,128)S(1)} %get-tuple-element.45), channel_id=1, source_target_pairs={{0,4},{1,5},{2,6},{3,7},{4,0},{5,1},{6,2},{7,3},{8,12},{9,13},{10,... | collective-permute-start | bytes 786440 | tf_op jit(solution)/shard_map/ppermute | solution.py:240
  55.3 20.5 %collective-permute-start.11 = (f32[1024,128]{1,0:T(8,128)}, f32[1024,128]{1,0:T(8,128)}, u32[]{:S(2)}, u32[]{:S(2)}) collective-permute-start(f32[1024,128]{1,0:T(8,128)} %get-tuple-element.42), channel_id=1, source_target_pairs={{0,2},{1,3},{2,0},{3,1},{4,6},{5,7},{6,4},{7,5},{8,10},{9,11},{10,... | collective-permute-start | bytes 1572872 | tf_op jit(solution)/shard_map/ppermute | solution.py:240
  56.9 14.1 %collective-permute-start.4 = (f32[512,128]{1,0:T(8,128)S(1)}, f32[512,128]{1,0:T(8,128)S(1)}, u32[]{:S(2)}, u32[]{:S(2)}) collective-permute-start(f32[512,128]{1,0:T(8,128)S(1)} %add.80.refs_4_), channel_id=1, source_target_pairs={{0,8},{1,9},{2,10},{3,11},{4,12},{5,13},{6,14},{7,15},{8,0},{9,1},... | collective-permute-start | bytes 786440 | tf_op jit(solution)/shard_map/ppermute | solution.py:240
  60.6 12.7 %collective-permute-start.8 = (f32[512,128]{1,0:T(8,128)S(1)}, f32[512,128]{1,0:T(8,128)}, u32[]{:S(2)}, u32[]{:S(2)}) collective-permute-start(f32[512,128]{1,0:T(8,128)S(1)} %get-tuple-element.43), channel_id=1, source_target_pairs={{0,4},{1,5},{2,6},{3,7},{4,0},{5,1},{6,2},{7,3},{8,12},{9,13},{10,... | collective-permute-start | bytes 786440 | tf_op jit(solution)/shard_map/ppermute | solution.py:240
  71.8 14.2 %collective-permute-start.7 = (f32[512,128]{1,0:T(8,128)}, f32[512,128]{1,0:T(8,128)}, u32[]{:S(2)}, u32[]{:S(2)}) collective-permute-start(f32[512,128]{1,0:T(8,128)} %shard_map.80), channel_id=1, source_target_pairs={{0,4},{1,5},{2,6},{3,7},{4,0},{5,1},{6,2},{7,3},{8,12},{9,13},{10,... | collective-permute-start | bytes 786440 | tf_op jit(solution)/shard_map/ppermute | solution.py:240
  73.3 12.7 %copy-start.15 = (f32[512,128]{1,0:T(8,128)S(1)}, f32[512,128]{1,0:T(8,128)}, u32[]{:S(2)}) copy-start(f32[512,128]{1,0:T(8,128)} %shard_map.80) | copy-start | bytes 786436
  74.4 13.4 %collective-permute-start.10 = (f32[512,128]{1,0:T(8,128)S(1)}, f32[512,128]{1,0:T(8,128)}, u32[]{:S(2)}, u32[]{:S(2)}) collective-permute-start(f32[512,128]{1,0:T(8,128)S(1)} %add.83.refs_1_), channel_id=1, source_target_pairs={{0,8},{1,9},{2,10},{3,11},{4,12},{5,13},{6,14},{7,15},{8,0},{9,1},... | collective-permute-start | bytes 786440 | tf_op jit(solution)/shard_map/ppermute | solution.py:240
  77.0 16.2 %copy-start.8 = (f32[1024,128]{1,0:T(8,128)S(1)}, f32[1024,128]{1,0:T(8,128)}, u32[]{:S(2)}) copy-start(f32[1024,128]{1,0:T(8,128)} %copy-done.7) | copy-start | bytes 1572868
  77.8 13.5 %collective-permute-start.12 = (f32[512,128]{1,0:T(8,128)S(1)}, f32[512,128]{1,0:T(8,128)}, u32[]{:S(2)}, u32[]{:S(2)}) collective-permute-start(f32[512,128]{1,0:T(8,128)S(1)} %dynamic-slice_bitcast_fusion), channel_id=1, source_target_pairs={{0,4},{1,5},{2,6},{3,7},{4,0},{5,1},{6,2},{7,3},{8,12},{9,13},{10,... | collective-permute-start | bytes 786440 | tf_op jit(solution)/shard_map/ppermute | solution.py:240
  77.9 15.3 %collective-permute-start.9 = (f32[1024,128]{1,0:T(8,128)}, f32[1024,128]{1,0:T(8,128)S(1)}, u32[]{:S(2)}, u32[]{:S(2)}) collective-permute-start(f32[1024,128]{1,0:T(8,128)} %shard_map.81), channel_id=1, source_target_pairs={{0,2},{1,3},{2,0},{3,1},{4,6},{5,7},{6,4},{7,5},{8,10},{9,11},{10,... | collective-permute-start | bytes 1572872 | tf_op jit(solution)/shard_map/ppermute | solution.py:240
  94.4 1.2 %collective-permute-start.13 = (f32[64,128]{1,0:T(8,128)S(1)}, f32[64,128]{1,0:T(8,128)S(1)}, u32[]{:S(2)}, u32[]{:S(2)}) collective-permute-start(f32[64,128]{1,0:T(8,128)S(1)} %reshape.72), channel_id=1, source_target_pairs={{0,1},{1,0},{2,3},{3,2},{4,5},{5,4},{6,7},{7,6},{8,9},{9,8},{10,11... | collective-permute-start | bytes 98312 | tf_op jit(solution)/shard_map/ppermute | solution.py:240
  95.6 5.7 %collective-permute-start.16 = (f32[64,128]{1,0:T(8,128)S(1)}, f32[64,128]{1,0:T(8,128)S(1)}, u32[]{:S(2)}, u32[]{:S(2)}) collective-permute-start(f32[64,128]{1,0:T(8,128)S(1)} %add.90), channel_id=1, source_target_pairs={{0,12},{1,13},{2,14},{3,15},{4,8},{5,9},{6,10},{7,11},{8,4},{9,5},... | collective-permute-start | bytes 98312 | tf_op jit(solution)/shard_map/ppermute | solution.py:240
  97.4 4.9 %collective-permute-start.15 = (f32[64,128]{1,0:T(8,128)S(1)}, f32[64,128]{1,0:T(8,128)S(1)}, u32[]{:S(2)}, u32[]{:S(2)}) collective-permute-start(f32[64,128]{1,0:T(8,128)S(1)} %add.90), channel_id=1, source_target_pairs={{0,8},{1,9},{2,10},{3,11},{4,12},{5,13},{6,14},{7,15},{8,0},{9,1},... | collective-permute-start | bytes 98312 | tf_op jit(solution)/shard_map/ppermute | solution.py:240
  97.4 5.0 %collective-permute-start.14 = (f32[64,128]{1,0:T(8,128)S(1)}, f32[64,128]{1,0:T(8,128)S(1)}, u32[]{:S(2)}, u32[]{:S(2)}) collective-permute-start(f32[64,128]{1,0:T(8,128)S(1)} %add.90), channel_id=1, source_target_pairs={{0,4},{1,5},{2,6},{3,7},{4,0},{5,1},{6,2},{7,3},{8,12},{9,13},{10,... | collective-permute-start | bytes 98312 | tf_op jit(solution)/shard_map/ppermute | solution.py:240
  102.5 4.0 %collective-permute-start.17 = (f32[64,128]{1,0:T(8,128)S(1)}, f32[64,128]{1,0:T(8,128)S(1)}, u32[]{:S(2)}, u32[]{:S(2)}) collective-permute-start(f32[64,128]{1,0:T(8,128)S(1)} %add_add_fusion), channel_id=1, source_target_pairs={{0,2},{1,3},{2,0},{3,1},{4,6},{5,7},{6,4},{7,5},{8,10},{9,11},{10,... | collective-permute-start | bytes 98312 | tf_op jit(solution)/shard_map/ppermute | solution.py:240
  (11 other events, 19.0 us)

commit v4 on v3

--- a/solution.py
+++ b/solution.py
@@ -12,7 +12,7 @@
 LANES = 128
 HALF = LANES // 2
 SLOTS = 4
-VMEM_LIMIT = 16 * 1024 * 1024
+VMEM_LIMIT = 12 * 1024 * 1024
 
 ANY = pl.BlockSpec(memory_space=pl.ANY)
 IN_HBM = pl.BlockSpec(memory_space=pltpu.HBM)

time: 108 us -> 109 us (level)
  transfers between devices with their start and end apart: 18 -> 18, of which waited for: 9 -> 10; matrix products, arithmetic and copies ran while one was open for 8% -> 8% of each run, Pallas kernels for 28% -> 28%
where the time goes in v4:
time: 109 us; the launch traced here: 108 us
  Pallas kernels  49.5 us (45%)
  starting transfers between devices  21.8 us (20%)
  waiting for transfers between devices  19 us (17%)
  local copies, waits for them, and re-layouts  7.04 us (6%)
  other arithmetic  6.31 us (6%)
  matrix products  4.06 us (4%)
    pallas_call x5, Pallas kernels, project(): pl.pallas_call(functools.partial(project_kernel, tile, cuts, add is not N...  47.9 us
    ppermute x18, starting transfers between devices, swap(): return lax.ppermute(value, 'store', [(i, i ^ bit) for i in range(16)])  21.8 us
    ppermute x18, waiting for transfers between devices, swap(): return lax.ppermute(value, 'store', [(i, i ^ bit) for i in range(16)])  19 us
    unnamed x34, local copies, waits for them, and re-layouts  5.66 us
    dot_general x2, matrix products, contract(): lax.dot_general(left, right, (((0,), (0,)), ((), ())), precision=lax.Prec...  2.81 us
  transfers between devices with their start and end apart: 18, of which 10 were waited for; matrix products, arithmetic and copies ran while one was open for 8% of the time, Pallas kernels for 28%

profile of v4, /device:TPU:0, one launch (start us, length us, event | category | flops | bytes accessed | tf_op | source)
XLA Modules:
  0.0 107.9 jit_solution(14863627297125256098)
XLA Ops:
  0.1 11.0 %shard_map.73 = (f32[4096,128]{1,0:T(8,128)}, bf16[2,512,128]{2,1,0:T(8,128)(2,1)S(1)}) custom-call(s32[6]{0:T(128)S(1)} %stack.68.refs_0_, bf16[16384,512]{1,0:T(8,128)(2,1)} %refs_1_.6, s32[8,32]{1,0:T(8,128)} %refs_2_.1, bf16[256,8,32]{2,1,0:T(8,128)(2,1)} %bitcast.49), custom_call_target="tpu_custom_call" | custom-call | flops 268435456 | bytes 2097152 | tf_op jit(solution)/shard_map/pallas_call | solution.py:196
  12.2 1.6 %shard_map.74.refs_4_.refs_2_ = bf16[2,1792,128]{2,1,0:T(8,128)(2,1)S(1)} custom-call(s32[1]{0:T(128)} %bitcast.6.first_ref, s32[8,112]{1,0:T(8,128)S(1)} %copy-done.13, bf16[8,256,112]{2,1,0:T(8,128)(2,1)S(1)} %bitcast.42, f32[4096,128]{1,0:T(8,128)} %get-tuple-element.24.rest_0_), custom_call_target="tpu_custom_call" | custom-call | flops 1000000000 | bytes 458752 | tf_op jit(solution)/shard_map/pallas_call | solution.py:85
  13.8 2.4 %collective-permute-done.refs_3_ = f32[4096,128]{1,0:T(8,128)} collective-permute-done((f32[4096,128]{1,0:T(8,128)}, f32[4096,128]{1,0:T(8,128)}, u32[]{:S(2)}, u32[]{:S(2)}) %collective-permute-start) | collective-permute-done | bytes 2097184 | tf_op jit(solution)/shard_map/ppermute | solution.py:240
  16.3 7.8 %shard_map.75 = (f32[1024,128]{1,0:T(8,128)S(1)}, f32[1024,128]{1,0:T(8,128)S(1)}, f32[1024,128]{1,0:T(8,128)S(1)}, f32[1024,128]{1,0:T(8,128)S(1)}) custom-call(s32[6]{0:T(128)S(1)} %stack.66.refs_0_, bf16[16384,512]{1,0:T(8,128)(2,1)} %refs_1_.6, bf16[2,512,128]{2,1,0:T(8,128)(2,1)S(1)} %copy-done.10, f32[4096,128]{1,0:T(8,128)} %collective-permute-done.refs_3_, ...), custom_call_target="tpu_custom_call" | custom-call | flops 268435456 | bytes 2097152 | tf_op jit(solution)/shard_map/pallas_call | solution.py:196
  24.1 3.0 %collective-permute-start.1 = (f32[1024,128]{1,0:T(8,128)S(1)}, f32[1024,128]{1,0:T(8,128)S(1)}, u32[]{:S(2)}, u32[]{:S(2)}) collective-permute-start(f32[1024,128]{1,0:T(8,128)S(1)} %get-tuple-element.31), channel_id=1, source_target_pairs={{0,2},{1,3},{2,0},{3,1},{4,6},{5,7},{6,4},{7,5},{8,10},{9,11},{10,... | collective-permute-start | bytes 1572872 | tf_op jit(solution)/shard_map/ppermute | solution.py:240
  27.1 12.5 %shard_map.76 = (f32[2048,128]{1,0:T(8,128)S(1)}, f32[2048,128]{1,0:T(8,128)S(1)}, f32[1024,128]{1,0:T(8,128)S(1)}) custom-call(s32[6]{0:T(128)S(1)} %stack.68.refs_0_, bf16[16384,1792]{1,0:T(8,128)(2,1)} %refs_1_.9, bf16[2,1792,128]{2,1,0:T(8,128)(2,1)S(1)} %shard_map.74.refs_4_.refs_2_, ...), custom_call_target="tpu_custom_call", output_to_operand_aliasing={{2}: (4, {})} | custom-call | flops 939524096 | bytes 7340032 | tf_op jit(solution)/shard_map/pallas_call | solution.py:196
  43.5 2.1 %collective-permute-start.3 = (f32[512,128]{1,0:T(8,128)S(1)}, f32[512,128]{1,0:T(8,128)S(1)}, u32[]{:S(2)}, u32[]{:S(2)}) collective-permute-start(f32[512,128]{1,0:T(8,128)S(1)} %get-tuple-element.45), channel_id=1, source_target_pairs={{0,4},{1,5},{2,6},{3,7},{4,0},{5,1},{6,2},{7,3},{8,12},{9,13},{10,... | collective-permute-start | bytes 786440 | tf_op jit(solution)/shard_map/ppermute | solution.py:240
  45.6 1.2 %copy-done.2 = f32[2048,128]{1,0:T(8,128)S(1)} copy-done((f32[2048,128]{1,0:T(8,128)S(1)}, f32[2048,128]{1,0:T(8,128)}, u32[]{:S(2)}) %copy-start.2) | copy-done | bytes 1048600
  46.8 8.5 %shard_map.78 = (f32[1024,128]{1,0:T(8,128)}, f32[1024,128]{1,0:T(8,128)S(1)}, f32[512,128]{1,0:T(8,128)S(1)}, f32[1024,128]{1,0:T(8,128)S(1)}) custom-call(s32[6]{0:T(128)S(1)} %stack.66.refs_0_, bf16[16384,1792]{1,0:T(8,128)(2,1)} %refs_1_.9, bf16[2,1792,128]{2,1,0:T(8,128)(2,1)S(1)} %shard_map.74.refs_4_.refs_2_, ...), custom_call_target="tpu_custom_call", output_to_operand_aliasing={{2}: (5, {}), {3}: (6, {})} | custom-call | flops 469762048 | bytes 3670016 | tf_op jit(solution)/shard_map/pallas_call | solution.py:196
  55.3 1.6 %collective-permute-start.11 = (f32[1024,128]{1,0:T(8,128)}, f32[1024,128]{1,0:T(8,128)}, u32[]{:S(2)}, u32[]{:S(2)}) collective-permute-start(f32[1024,128]{1,0:T(8,128)} %get-tuple-element.42), channel_id=1, source_target_pairs={{0,2},{1,3},{2,0},{3,1},{4,6},{5,7},{6,4},{7,5},{8,10},{9,11},{10,... | collective-permute-start | bytes 1572872 | tf_op jit(solution)/shard_map/ppermute | solution.py:240
  56.9 2.6 %collective-permute-start.4 = (f32[512,128]{1,0:T(8,128)S(1)}, f32[512,128]{1,0:T(8,128)S(1)}, u32[]{:S(2)}, u32[]{:S(2)}) collective-permute-start(f32[512,128]{1,0:T(8,128)S(1)} %add.80.refs_4_), channel_id=1, source_target_pairs={{0,8},{1,9},{2,10},{3,11},{4,12},{5,13},{6,14},{7,15},{8,0},{9,1},... | collective-permute-start | bytes 786440 | tf_op jit(solution)/shard_map/ppermute | solution.py:240
  61.3 8.1 %shard_map.79 = (f32[1024,128]{1,0:T(8,128)S(1)}, f32[1024,128]{1,0:T(8,128)S(1)}, f32[1024,128]{1,0:T(8,128)S(1)}, f32[512,128]{1,0:T(8,128)S(1)}) custom-call(s32[6]{0:T(128)S(1)} %stack.66.refs_0_, bf16[16384,1792]{1,0:T(8,128)(2,1)} %refs_1_.9, ...), custom_call_target="tpu_custom_call", output_to_operand_aliasing={{2}: (5, {}), {3}: (6, {})} | custom-call | flops 469762048 | bytes 3670016 | tf_op jit(solution)/shard_map/pallas_call | solution.py:196
  71.9 1.5 %collective-permute-start.7 = (f32[512,128]{1,0:T(8,128)}, f32[512,128]{1,0:T(8,128)}, u32[]{:S(2)}, u32[]{:S(2)}) collective-permute-start(f32[512,128]{1,0:T(8,128)} %shard_map.80), channel_id=1, source_target_pairs={{0,4},{1,5},{2,6},{3,7},{4,0},{5,1},{6,2},{7,3},{8,12},{9,13},{10,... | collective-permute-start | bytes 786440 | tf_op jit(solution)/shard_map/ppermute | solution.py:240
  74.5 1.3 %collective-permute-start.10 = (f32[512,128]{1,0:T(8,128)S(1)}, f32[512,128]{1,0:T(8,128)}, u32[]{:S(2)}, u32[]{:S(2)}) collective-permute-start(f32[512,128]{1,0:T(8,128)S(1)} %add.83.refs_1_), channel_id=1, source_target_pairs={{0,8},{1,9},{2,10},{3,11},{4,12},{5,13},{6,14},{7,15},{8,0},{9,1},... | collective-permute-start | bytes 786440 | tf_op jit(solution)/shard_map/ppermute | solution.py:240
  77.8 1.6 %collective-permute-start.9 = (f32[1024,128]{1,0:T(8,128)}, f32[1024,128]{1,0:T(8,128)S(1)}, u32[]{:S(2)}, u32[]{:S(2)}) collective-permute-start(f32[1024,128]{1,0:T(8,128)} %shard_map.81), channel_id=1, source_target_pairs={{0,2},{1,3},{2,0},{3,1},{4,6},{5,7},{6,4},{7,5},{8,10},{9,11},{10,... | collective-permute-start | bytes 1572872 | tf_op jit(solution)/shard_map/ppermute | solution.py:240
  79.5 6.4 %collective-permute-done.7 = f32[512,128]{1,0:T(8,128)} collective-permute-done((f32[512,128]{1,0:T(8,128)}, f32[512,128]{1,0:T(8,128)}, u32[]{:S(2)}, u32[]{:S(2)}) %collective-permute-start.7) | collective-permute-done | bytes 262176 | tf_op jit(solution)/shard_map/ppermute | solution.py:240
  87.9 3.5 %collective-permute-done.12 = f32[512,128]{1,0:T(8,128)} collective-permute-done((f32[512,128]{1,0:T(8,128)S(1)}, f32[512,128]{1,0:T(8,128)}, u32[]{:S(2)}, u32[]{:S(2)}) %collective-permute-start.12) | collective-permute-done | bytes 262176 | tf_op jit(solution)/shard_map/ppermute | solution.py:240
  91.4 1.8 %fusion.2 = f32[128,128]{1,0:T(8,128)S(1)} fusion(f32[512,128]{1,0:T(8,128)} %collective-permute-done.12, f32[2,512,128]{2,1,0:T(8,128)} %bitcast.47, s32[]{:T(128)S(6)} %select_n.84, f32[512,128]{1,0:T(8,128)} %copy-done.14, f32[512,128]{1,0:T(8,128)} %collective-permute-done.10), kind=kOutput, calls=%fused_computation.4 | convolution fusion | flops 100794368 | bytes 1114116 | tf_op jit(solution)/shard_map/dot_general | solution.py:225
  95.7 1.6 %collective-permute-start.16 = (f32[64,128]{1,0:T(8,128)S(1)}, f32[64,128]{1,0:T(8,128)S(1)}, u32[]{:S(2)}, u32[]{:S(2)}) collective-permute-start(f32[64,128]{1,0:T(8,128)S(1)} %add.90), channel_id=1, source_target_pairs={{0,12},{1,13},{2,14},{3,15},{4,8},{5,9},{6,10},{7,11},{8,4},{9,5},... | collective-permute-start | bytes 98312 | tf_op jit(solution)/shard_map/ppermute | solution.py:240
  97.5 2.6 %collective-permute-start.14 = (f32[64,128]{1,0:T(8,128)S(1)}, f32[64,128]{1,0:T(8,128)S(1)}, u32[]{:S(2)}, u32[]{:S(2)}) collective-permute-start(f32[64,128]{1,0:T(8,128)S(1)} %add.90), channel_id=1, source_target_pairs={{0,4},{1,5},{2,6},{3,7},{4,0},{5,1},{6,2},{7,3},{8,12},{9,13},{10,... | collective-permute-start | bytes 98312 | tf_op jit(solution)/shard_map/ppermute | solution.py:240
  100.1 1.3 %collective-permute-done.16 = f32[64,128]{1,0:T(8,128)S(1)} collective-permute-done((f32[64,128]{1,0:T(8,128)S(1)}, f32[64,128]{1,0:T(8,128)S(1)}, u32[]{:S(2)}, u32[]{:S(2)}) %collective-permute-start.16) | collective-permute-done | bytes 32800 | tf_op jit(solution)/shard_map/ppermute | solution.py:240
  102.6 2.0 %collective-permute-start.17 = (f32[64,128]{1,0:T(8,128)S(1)}, f32[64,128]{1,0:T(8,128)S(1)}, u32[]{:S(2)}, u32[]{:S(2)}) collective-permute-start(f32[64,128]{1,0:T(8,128)S(1)} %add_add_fusion), channel_id=1, source_target_pairs={{0,2},{1,3},{2,0},{3,1},{4,6},{5,7},{6,4},{7,5},{8,10},{9,11},{10,... | collective-permute-start | bytes 98312 | tf_op jit(solution)/shard_map/ppermute | solution.py:240
  104.6 1.9 %collective-permute-done.17 = f32[64,128]{1,0:T(8,128)S(1)} collective-permute-done((f32[64,128]{1,0:T(8,128)S(1)}, f32[64,128]{1,0:T(8,128)S(1)}, u32[]{:S(2)}, u32[]{:S(2)}) %collective-permute-start.17) | collective-permute-done | bytes 32800 | tf_op jit(solution)/shard_map/ppermute | solution.py:240
  106.7 1.2 %fusion.9 = f32[4,256]{1,0:T(4,128)} fusion(bf16[4,4096]{1,0:T(4,128)(2,1)S(1)} %convert_element_type.7, bf16[256,4096]{1,0:T(8,128)(2,1)S(1)} %copy-done), kind=kOutput, calls=%fused_computation.23 | convolution fusion | flops 8388608 | bytes 2134016 | tf_op jit(solution)/shard_map/dot_general | solution.py:356
  (79 shorter events, 18.5 us)
Async XLA Ops:
  0.0 106.7 %copy-start = (bf16[256,4096]{1,0:T(8,128)(2,1)S(1)}, bf16[256,4096]{1,0:T(8,128)(2,1)}, u32[]{:S(2)}) copy-start(bf16[256,4096]{1,0:T(8,128)(2,1)} %param.13) | copy-start | bytes 6291460
  0.1 12.2 %copy-start.11 = (bf16[8,112,32,8]{1,3,2,0:T(8,128)(2,1)S(1)}, bf16[8,112,32,8]{1,3,2,0:T(8,128)(2,1)}, u32[]{:S(2)}) copy-start(bf16[8,112,32,8]{1,3,2,0:T(8,128)(2,1)} %param.12) | copy-start | bytes 1376260
  0.1 12.2 %copy-start.13 = (s32[8,112]{1,0:T(8,128)S(1)}, s32[8,112]{1,0:T(8,128)}, u32[]{:S(2)}) copy-start(s32[8,112]{1,0:T(8,128)} %index_ref.1) | copy-start | bytes 10756
  11.8 4.5 %collective-permute-start = (f32[4096,128]{1,0:T(8,128)}, f32[4096,128]{1,0:T(8,128)}, u32[]{:S(2)}, u32[]{:S(2)}) collective-permute-start(f32[4096,128]{1,0:T(8,128)} %get-tuple-element.24.rest_0_), channel_id=1, source_target_pairs={{0,1},{1,0},{2,3},{3,2},{4,5},{5,4},{6,7},{7,6},{8,9},{9,8},{10,11... | collective-permute-start | bytes 6291464 | tf_op jit(solution)/shard_map/ppermute | solution.py:240
  24.1 15.5 %copy-start.12 = (f32[1024,128]{1,0:T(8,128)}, f32[1024,128]{1,0:T(8,128)S(1)}, u32[]{:S(2)}) copy-start(f32[1024,128]{1,0:T(8,128)S(1)} %get-tuple-element.37) | copy-start | bytes 1572868
  24.1 16.5 %collective-permute-start.1 = (f32[1024,128]{1,0:T(8,128)S(1)}, f32[1024,128]{1,0:T(8,128)S(1)}, u32[]{:S(2)}, u32[]{:S(2)}) collective-permute-start(f32[1024,128]{1,0:T(8,128)S(1)} %get-tuple-element.31), channel_id=1, source_target_pairs={{0,2},{1,3},{2,0},{3,1},{4,6},{5,7},{6,4},{7,5},{8,10},{9,11},{10,... | collective-permute-start | bytes 1572872 | tf_op jit(solution)/shard_map/ppermute | solution.py:240
  41.8 3.7 %collective-permute-start.2 = (f32[2048,128]{1,0:T(8,128)}, f32[2048,128]{1,0:T(8,128)}, u32[]{:S(2)}, u32[]{:S(2)}) collective-permute-start(f32[2048,128]{1,0:T(8,128)} %get-tuple-element.32), channel_id=1, source_target_pairs={{0,1},{1,0},{2,3},{3,2},{4,5},{5,4},{6,7},{7,6},{8,9},{9,8},{10,11... | collective-permute-start | bytes 3145736 | tf_op jit(solution)/shard_map/ppermute | solution.py:240
  41.8 19.4 %collective-permute-start.5 = (f32[2048,128]{1,0:T(8,128)}, f32[2048,128]{1,0:T(8,128)}, u32[]{:S(2)}, u32[]{:S(2)}) collective-permute-start(f32[2048,128]{1,0:T(8,128)} %get-tuple-element.33.refs_4_), channel_id=1, source_target_pairs={{0,1},{1,0},{2,3},{3,2},{4,5},{5,4},{6,7},{7,6},{8,9},{9,8},{10,11... | collective-permute-start | bytes 3145736 | tf_op jit(solution)/shard_map/ppermute | solution.py:240
  42.4 17.2 %collective-permute-start.6 = (f32[1024,128]{1,0:T(8,128)}, f32[1024,128]{1,0:T(8,128)}, u32[]{:S(2)}, u32[]{:S(2)}) collective-permute-start(f32[1024,128]{1,0:T(8,128)} %copy-done.12), channel_id=1, source_target_pairs={{0,2},{1,3},{2,0},{3,1},{4,6},{5,7},{6,4},{7,5},{8,10},{9,11},{10,... | collective-permute-start | bytes 1572872 | tf_op jit(solution)/shard_map/ppermute | solution.py:240
  43.5 13.4 %collective-permute-start.3 = (f32[512,128]{1,0:T(8,128)S(1)}, f32[512,128]{1,0:T(8,128)S(1)}, u32[]{:S(2)}, u32[]{:S(2)}) collective-permute-start(f32[512,128]{1,0:T(8,128)S(1)} %get-tuple-element.45), channel_id=1, source_target_pairs={{0,4},{1,5},{2,6},{3,7},{4,0},{5,1},{6,2},{7,3},{8,12},{9,13},{10,... | collective-permute-start | bytes 786440 | tf_op jit(solution)/shard_map/ppermute | solution.py:240
  55.3 20.5 %collective-permute-start.11 = (f32[1024,128]{1,0:T(8,128)}, f32[1024,128]{1,0:T(8,128)}, u32[]{:S(2)}, u32[]{:S(2)}) collective-permute-start(f32[1024,128]{1,0:T(8,128)} %get-tuple-element.42), channel_id=1, source_target_pairs={{0,2},{1,3},{2,0},{3,1},{4,6},{5,7},{6,4},{7,5},{8,10},{9,11},{10,... | collective-permute-start | bytes 1572872 | tf_op jit(solution)/shard_map/ppermute | solution.py:240
  56.9 14.1 %collective-permute-start.4 = (f32[512,128]{1,0:T(8,128)S(1)}, f32[512,128]{1,0:T(8,128)S(1)}, u32[]{:S(2)}, u32[]{:S(2)}) collective-permute-start(f32[512,128]{1,0:T(8,128)S(1)} %add.80.refs_4_), channel_id=1, source_target_pairs={{0,8},{1,9},{2,10},{3,11},{4,12},{5,13},{6,14},{7,15},{8,0},{9,1},... | collective-permute-start | bytes 786440 | tf_op jit(solution)/shard_map/ppermute | solution.py:240
  60.7 12.8 %collective-permute-start.8 = (f32[512,128]{1,0:T(8,128)S(1)}, f32[512,128]{1,0:T(8,128)}, u32[]{:S(2)}, u32[]{:S(2)}) collective-permute-start(f32[512,128]{1,0:T(8,128)S(1)} %get-tuple-element.43), channel_id=1, source_target_pairs={{0,4},{1,5},{2,6},{3,7},{4,0},{5,1},{6,2},{7,3},{8,12},{9,13},{10,... | collective-permute-start | bytes 786440 | tf_op jit(solution)/shard_map/ppermute | solution.py:240
  71.9 14.0 %collective-permute-start.7 = (f32[512,128]{1,0:T(8,128)}, f32[512,128]{1,0:T(8,128)}, u32[]{:S(2)}, u32[]{:S(2)}) collective-permute-start(f32[512,128]{1,0:T(8,128)} %shard_map.80), channel_id=1, source_target_pairs={{0,4},{1,5},{2,6},{3,7},{4,0},{5,1},{6,2},{7,3},{8,12},{9,13},{10,... | collective-permute-start | bytes 786440 | tf_op jit(solution)/shard_map/ppermute | solution.py:240
  73.5 12.4 %copy-start.15 = (f32[512,128]{1,0:T(8,128)S(1)}, f32[512,128]{1,0:T(8,128)}, u32[]{:S(2)}) copy-start(f32[512,128]{1,0:T(8,128)} %shard_map.80) | copy-start | bytes 786436
  74.5 13.4 %collective-permute-start.10 = (f32[512,128]{1,0:T(8,128)S(1)}, f32[512,128]{1,0:T(8,128)}, u32[]{:S(2)}, u32[]{:S(2)}) collective-permute-start(f32[512,128]{1,0:T(8,128)S(1)} %add.83.refs_1_), channel_id=1, source_target_pairs={{0,8},{1,9},{2,10},{3,11},{4,12},{5,13},{6,14},{7,15},{8,0},{9,1},... | collective-permute-start | bytes 786440 | tf_op jit(solution)/shard_map/ppermute | solution.py:240
  76.9 16.3 %copy-start.8 = (f32[1024,128]{1,0:T(8,128)S(1)}, f32[1024,128]{1,0:T(8,128)}, u32[]{:S(2)}) copy-start(f32[1024,128]{1,0:T(8,128)} %copy-done.7) | copy-start | bytes 1572868
  77.7 13.6 %collective-permute-start.12 = (f32[512,128]{1,0:T(8,128)S(1)}, f32[512,128]{1,0:T(8,128)}, u32[]{:S(2)}, u32[]{:S(2)}) collective-permute-start(f32[512,128]{1,0:T(8,128)S(1)} %dynamic-slice_bitcast_fusion), channel_id=1, source_target_pairs={{0,4},{1,5},{2,6},{3,7},{4,0},{5,1},{6,2},{7,3},{8,12},{9,13},{10,... | collective-permute-start | bytes 786440 | tf_op jit(solution)/shard_map/ppermute | solution.py:240
  77.8 15.4 %collective-permute-start.9 = (f32[1024,128]{1,0:T(8,128)}, f32[1024,128]{1,0:T(8,128)S(1)}, u32[]{:S(2)}, u32[]{:S(2)}) collective-permute-start(f32[1024,128]{1,0:T(8,128)} %shard_map.81), channel_id=1, source_target_pairs={{0,2},{1,3},{2,0},{3,1},{4,6},{5,7},{6,4},{7,5},{8,10},{9,11},{10,... | collective-permute-start | bytes 1572872 | tf_op jit(solution)/shard_map/ppermute | solution.py:240
  94.5 1.2 %collective-permute-start.13 = (f32[64,128]{1,0:T(8,128)S(1)}, f32[64,128]{1,0:T(8,128)S(1)}, u32[]{:S(2)}, u32[]{:S(2)}) collective-permute-start(f32[64,128]{1,0:T(8,128)S(1)} %reshape.72), channel_id=1, source_target_pairs={{0,1},{1,0},{2,3},{3,2},{4,5},{5,4},{6,7},{7,6},{8,9},{9,8},{10,11... | collective-permute-start | bytes 98312 | tf_op jit(solution)/shard_map/ppermute | solution.py:240
  95.7 5.7 %collective-permute-start.16 = (f32[64,128]{1,0:T(8,128)S(1)}, f32[64,128]{1,0:T(8,128)S(1)}, u32[]{:S(2)}, u32[]{:S(2)}) collective-permute-start(f32[64,128]{1,0:T(8,128)S(1)} %add.90), channel_id=1, source_target_pairs={{0,12},{1,13},{2,14},{3,15},{4,8},{5,9},{6,10},{7,11},{8,4},{9,5},... | collective-permute-start | bytes 98312 | tf_op jit(solution)/shard_map/ppermute | solution.py:240
  97.2 5.2 %collective-permute-start.15 = (f32[64,128]{1,0:T(8,128)S(1)}, f32[64,128]{1,0:T(8,128)S(1)}, u32[]{:S(2)}, u32[]{:S(2)}) collective-permute-start(f32[64,128]{1,0:T(8,128)S(1)} %add.90), channel_id=1, source_target_pairs={{0,8},{1,9},{2,10},{3,11},{4,12},{5,13},{6,14},{7,15},{8,0},{9,1},... | collective-permute-start | bytes 98312 | tf_op jit(solution)/shard_map/ppermute | solution.py:240
  97.5 5.0 %collective-permute-start.14 = (f32[64,128]{1,0:T(8,128)S(1)}, f32[64,128]{1,0:T(8,128)S(1)}, u32[]{:S(2)}, u32[]{:S(2)}) collective-permute-start(f32[64,128]{1,0:T(8,128)S(1)} %add.90), channel_id=1, source_target_pairs={{0,4},{1,5},{2,6},{3,7},{4,0},{5,1},{6,2},{7,3},{8,12},{9,13},{10,... | collective-permute-start | bytes 98312 | tf_op jit(solution)/shard_map/ppermute | solution.py:240
  102.6 4.0 %collective-permute-start.17 = (f32[64,128]{1,0:T(8,128)S(1)}, f32[64,128]{1,0:T(8,128)S(1)}, u32[]{:S(2)}, u32[]{:S(2)}) collective-permute-start(f32[64,128]{1,0:T(8,128)S(1)} %add_add_fusion), channel_id=1, source_target_pairs={{0,2},{1,3},{2,0},{3,1},{4,6},{5,7},{6,4},{7,5},{8,10},{9,11},{10,... | collective-permute-start | bytes 98312 | tf_op jit(solution)/shard_map/ppermute | solution.py:240
  (11 other events, 18.8 us)
